TPU v7x, 32 devices: a whole 2x2x4 slice. The times are simulated.
32 devices in a mesh: dp: 16 (over z, y, x), tensor: 2 (over core).
Axes of the slice: x: 2, y: 2, z: 4, core: 2. Of those that a mesh axis runs over, the one named last changes fastest.
Arguments:
- tokens: float32 [16384, 768], P(('dp', 'tensor')), may hold values from -6 to 6
- offsets: int32 [16, 16], P('dp'), may hold values from 0 to 1024, as said below
- w_qkv: bfloat16 [768, 3, 768], P('dp', None, 'tensor'), may hold values from -0.21875 to 0.21875
- w_attn_out: bfloat16 [768, 768], P('tensor', 'dp'), may hold values from -1.75 to 1.75
- w_in: bfloat16 [768, 2, 1152], P('dp', None, 'tensor'), may hold values from -0.21875 to 0.21875
- w_mlp_out: bfloat16 [1152, 768], P('tensor', 'dp'), may hold values from -0.1875 to 0.1875
- gain_attn: bfloat16 [768], P('dp'), may hold values from 0.099609375 to 1.8984375
- gain_mlp: bfloat16 [768], P('dp'), may hold values from 0.099609375 to 1.8984375
- cotangent: float32 [16384, 768], P(('dp', 'tensor')), may hold values from -6 to 6
Outputs:
- outputs: float32 [16384, 768], P(('dp', 'tensor'))
- grad_tokens: float32 [16384, 768], P(('dp', 'tensor'))
- grad_w_qkv: float32 [768, 3, 768], P('dp', None, 'tensor')
- grad_w_attn_out: float32 [768, 768], P('tensor', 'dp')
- grad_w_in: float32 [768, 2, 1152], P('dp', None, 'tensor')
- grad_w_mlp_out: float32 [1152, 768], P('tensor', 'dp')
- grad_gain_attn: float32 [768], P('dp')
- grad_gain_mlp: float32 [768], P('dp')
Inputs may be any that keep to these rules, and one draw needn't show every extreme that they name: `offsets`: each row holds the first tokens of 16 sequences of one group of 1024 tokens, rising from 0 and never falling (equal entries are empty sequences); a sequence ends where the next begins, the last at 1024. No sequence has more than 512 tokens; in every row one has exactly 512 and holds the group's tokens 512 - 1 and 512.
All inputs are finite; a program needn't handle non-finite values.
Results may differ from a plain program's by a relative error of at most 0.018.
Values may be sent and summed in bfloat16 or wider, within the bound.
A program may use at most 128 MiB of HBM per device.

v0:
```python
import functools
import math
import types

import jax
import jax.numpy as jnp
from jax import lax
from jax.experimental import pallas as pl
from jax.experimental.pallas import tpu as pltpu
from jax.sharding import PartitionSpec as P

HEAD_DIM = 64


EPSILON = 1e-05
ROPE_BASE = 160000.0
NEGATIVE = -1e30
LANES = 128
QUERY_BLOCK = 256
SCALE = 1.0 / math.sqrt(HEAD_DIM)
VMEM_LIMIT = 48 * 1024 * 1024


def seq_starts(offset_row, position):
    before = offset_row[None, :] <= position[:, None]
    return jnp.max(jnp.where(before, offset_row[None, :], 0), axis=1)


def rope_tables(position):
    half_dim = HEAD_DIM // 2
    inverse = jnp.power(
        jnp.float32(ROPE_BASE), -2.0 * jnp.arange(half_dim, dtype=jnp.float32) / HEAD_DIM
    )
    angles = position.astype(jnp.float32)[:, None] * inverse[None, :]
    copies = LANES // half_dim
    cosine = jnp.cos(angles)
    sine = jnp.sin(angles)
    return (
        jnp.concatenate([cosine] * copies, axis=1),
        jnp.concatenate([-sine, sine] * (copies // 2), axis=1),
    )


def levels_of(count):
    out = []
    stride = 1
    while stride < count:
        size = min(4, count // stride)
        out.append((stride, size))
        stride *= size
    return out


def swap_pairs(count, mask):
    return [(place, place ^ mask) for place in range(count)]


def send_step(held, stride, size):
    count = lax.axis_size("dp")
    return [held] + [
        lax.ppermute(held, "dp", swap_pairs(count, step * stride)) for step in range(1, size)
    ]


def place_step(taken, stride, size):
    mine = (lax.axis_index("dp") // stride) % size
    outer, height, width = taken[0].shape
    spread = jnp.zeros((outer, size, height, width), taken[0].dtype)
    for step in range(size):
        spread = lax.dynamic_update_slice(spread, taken[step][:, None], (0, mine ^ step, 0, 0))
    return spread.reshape(outer * size, height, width)


def after(later, *earlier):
    return lax.optimization_barrier((later, *earlier))[0]


def gather_both(first, second):
    one, two = first[None], second[None]
    taken = None
    for level in reversed(levels_of(lax.axis_size("dp"))):
        if taken is not None:
            two = place_step(taken, *last)
        one = place_step(send_step(one, *level), *level)
        taken = send_step(after(two, one), *level)
        last = level
    return one.reshape(-1, one.shape[2]), (taken, last)


def gather_rest(pending, *earlier):
    taken, level = pending
    taken = lax.optimization_barrier((taken, *earlier))[0]
    full = place_step(taken, *level)
    return full.reshape(-1, full.shape[2])


def sum_blocks(terms, *earlier):
    count = lax.axis_size("dp")
    me = lax.axis_index("dp")
    height = terms.shape[0] // count
    width = terms.shape[1]
    held = terms
    for stride, size in levels_of(count):
        mine = (me // stride) % size
        parts = held.reshape(-1, size, height, width)
        pick = lambda place: lax.dynamic_index_in_dim(parts, place, 1, keepdims=False)
        got = [
            lax.ppermute(pick(mine ^ step), "dp", swap_pairs(count, step * stride))
            for step in range(1, size)
        ]
        if earlier:
            got = lax.optimization_barrier((got, *earlier))[0]
            earlier = ()
        total = pick(mine).astype(jnp.float32)
        for other in got:
            total = total + other.astype(jnp.float32)
        held = total.astype(jnp.bfloat16)
    return total.reshape(height, width)


def other_half(local_rows):
    return lax.ppermute(local_rows, "tensor", [(0, 1), (1, 0)])


def spread_rows(local_rows):
    return jnp.concatenate([local_rows, other_half(local_rows)], axis=0)


def collect_own(partial_sums, rows_here):
    sent = other_half(partial_sums[rows_here:].astype(jnp.bfloat16))
    return partial_sums[:rows_here] + sent.astype(jnp.float32)


def collect_all(partial_sums, rows_here):
    got = other_half(partial_sums.astype(jnp.bfloat16))
    swapped = jnp.concatenate([got[rows_here:], got[:rows_here]], axis=0)
    return partial_sums + swapped.astype(jnp.float32)


def norm_parts(inputs_v):
    centre = inputs_v - jnp.mean(inputs_v, axis=-1, keepdims=True)
    spread = jnp.mean(centre * centre, axis=-1, keepdims=True)
    scale_v = lax.rsqrt(spread + EPSILON)
    return centre * scale_v, scale_v


def norm_backward(incoming, gain_v, unit, scale_v):
    scaled = incoming * gain_v
    mean_one = jnp.mean(scaled, axis=-1, keepdims=True)
    mean_two = jnp.mean(scaled * unit, axis=-1, keepdims=True)
    return scale_v * (scaled - mean_one - unit * mean_two)


def two_terms(column):
    high = column.astype(jnp.bfloat16)
    rest = (column - lax.reduce_precision(column, 8, 7)).astype(jnp.bfloat16)
    return jnp.stack([high, rest], axis=1)


def padded(pieces):
    width = sum(piece.shape[1] for piece in pieces)
    short = -width % 128
    height = pieces[0].shape[0]
    if short:
        pieces = pieces + [jnp.zeros((height, short), jnp.bfloat16)]
    return jnp.concatenate(pieces, axis=1)


def dot_nn(left, right):
    return jnp.dot(left, right, preferred_element_type=jnp.float32)


def dot_nt(left, right):
    return lax.dot_general(
        left, right, (((1,), (1,)), ((), ())), preferred_element_type=jnp.float32
    )


def dot_tn(left, right):
    return lax.dot_general(
        left, right, (((0,), (0,)), ((), ())), preferred_element_type=jnp.float32
    )


def turn(rows, cosine, sine_signed, lane):
    half_dim = HEAD_DIM // 2
    ahead = pltpu.roll(rows, rows.shape[1] - half_dim, axis=1)
    behind = pltpu.roll(rows, half_dim, axis=1)
    swapped = jnp.where(lane % HEAD_DIM < half_dim, ahead, behind)
    return rows * cosine + swapped * sine_signed


def forward_kernel(
    normed_ref, wq_ref, wk_ref, wv_ref, cos_ref, sin_ref, srow_ref, scol_ref,
    q_ref, k_ref, v_ref, ctx_ref, lse_ref, vt_ref,
):
    rows = normed_ref.shape[0]
    block = min(QUERY_BLOCK, rows)
    normed = normed_ref[...]
    cosine = cos_ref[...]
    sine = sin_ref[...]
    lane = lax.broadcasted_iota(jnp.int32, (rows, LANES), 1)
    dot = functools.partial(jnp.dot, preferred_element_type=jnp.float32)
    q_ref[...] = turn(dot(normed, wq_ref[...]), cosine, sine, lane).astype(jnp.bfloat16)
    k_ref[...] = turn(dot(normed, wk_ref[...]), cosine, sine, lane).astype(jnp.bfloat16)
    values = dot(normed, wv_ref[...])
    v_ref[...] = values.astype(jnp.bfloat16)
    vt_ref[...] = values.T.astype(jnp.bfloat16)

    @pl.loop(0, rows // block)
    def _(step):
        at = pl.ds(pl.multiple_of(step * block, block), block)
        same = scol_ref[...] == srow_ref[:, at]
        parts = []
        for head in range(LANES // HEAD_DIM):
            cols = slice(head * HEAD_DIM, (head + 1) * HEAD_DIM)
            scores = dot_nt(k_ref[:, cols], q_ref[at, cols]) * SCALE
            scores = jnp.where(same, scores, NEGATIVE)
            top = jnp.max(scores, axis=0, keepdims=True)
            terms = jnp.exp(scores - top)
            total = jnp.sum(terms, axis=0, keepdims=True)
            weights = (terms * (1.0 / total)).astype(jnp.bfloat16)
            parts.append(dot(vt_ref[cols, :], weights))
            lse_ref[0, head : head + 1, at] = top + jnp.log(total)
        ctx_ref[at, :] = jnp.concatenate(parts, axis=0).T.astype(jnp.bfloat16)


def backward_kernel(
    grad_ref, wo_ref, q_ref, k_ref, v_ref, cos_ref, sin_ref, srow_ref, scol_ref, lse_ref,
    dq_ref, dk_ref, dv_ref, g_ref, kt_ref, acc_q, acc_k, acc_v,
):
    rows = grad_ref.shape[0]
    block = min(QUERY_BLOCK, rows)
    dot = functools.partial(jnp.dot, preferred_element_type=jnp.float32)
    g_ref[...] = dot(grad_ref[...], wo_ref[...]).astype(jnp.bfloat16)
    kt_ref[...] = k_ref[...].astype(jnp.float32).T.astype(jnp.bfloat16)
    acc_k[...] = jnp.zeros_like(acc_k)
    acc_v[...] = jnp.zeros_like(acc_v)

    @pl.loop(0, rows // block)
    def _(step):
        at = pl.ds(pl.multiple_of(step * block, block), block)
        same = scol_ref[...] == srow_ref[:, at]
        parts = []
        for head in range(LANES // HEAD_DIM):
            cols = slice(head * HEAD_DIM, (head + 1) * HEAD_DIM)
            query = q_ref[at, cols]
            grad = g_ref[at, cols]
            scores = dot_nt(k_ref[:, cols], query) * SCALE
            probs = jnp.exp(jnp.where(same, scores - lse_ref[0, head : head + 1, at], NEGATIVE))
            acc_v[:, cols] += dot(probs.astype(jnp.bfloat16), grad)
            grad_probs = dot_nt(v_ref[:, cols], grad)
            weighted = probs * grad_probs
            drop = jnp.sum(weighted, axis=0, keepdims=True)
            grad_scores = (weighted - probs * drop).astype(jnp.bfloat16)
            acc_k[:, cols] += dot(grad_scores, query)
            parts.append(dot(kt_ref[cols, :], grad_scores))
        acc_q[at, :] = jnp.concatenate(parts, axis=0).T

    cosine = cos_ref[...] * SCALE
    sine = sin_ref[...] * -SCALE
    lane = lax.broadcasted_iota(jnp.int32, (rows, LANES), 1)
    dq_ref[...] = turn(acc_q[...], cosine, sine, lane).astype(jnp.bfloat16)
    dk_ref[...] = turn(acc_k[...], cosine, sine, lane).astype(jnp.bfloat16)
    dv_ref[...] = acc_v[...].astype(jnp.bfloat16)


def whole(shape):
    return pl.BlockSpec(shape, lambda pair: (0,) * len(shape))


def column_block(rows, first):
    return pl.BlockSpec((rows, LANES), lambda pair: (0, first + pair))


def attention_forward(normed_all, attn_pack, cosine, sine, starts, width_here):
    rows, width = normed_all.shape
    pairs = width_here // LANES
    heads_each = LANES // HEAD_DIM
    low = jax.ShapeDtypeStruct((rows, width_here), jnp.bfloat16)
    return pl.pallas_call(
        forward_kernel,
        grid=(pairs,),
        out_shape=(low, low, low, low, jax.ShapeDtypeStruct((pairs, heads_each, rows), jnp.float32)),
        in_specs=[
            whole((rows, width)),
            column_block(width, 0),
            column_block(width, pairs),
            column_block(width, 2 * pairs),
            whole((rows, LANES)),
            whole((rows, LANES)),
            whole((1, rows)),
            whole((rows, 1)),
        ],
        out_specs=[column_block(rows, 0)] * 4
        + [pl.BlockSpec((1, heads_each, rows), lambda pair: (pair, 0, 0))],
        scratch_shapes=[pltpu.VMEM((LANES, rows), jnp.bfloat16)],
        compiler_params=pltpu.CompilerParams(vmem_limit_bytes=VMEM_LIMIT),
        cost_estimate=pl.CostEstimate(
            flops=2 * rows * width * 3 * width_here + 4 * rows * rows * width_here,
            bytes_accessed=2 * (rows * width + 3 * width * width_here + 4 * rows * width_here),
            transcendentals=rows * rows * width_here // HEAD_DIM,
        ),
    )(normed_all, attn_pack, attn_pack, attn_pack, cosine, sine, starts[None, :], starts[:, None])


def attention_backward(grad_rows, attn_pack, queries, key_rows, values, cosine, sine, starts, lse):
    rows, width = grad_rows.shape
    width_here = queries.shape[1]
    pairs = width_here // LANES
    heads_each = LANES // HEAD_DIM
    low = jax.ShapeDtypeStruct((rows, width_here), jnp.bfloat16)
    return pl.pallas_call(
        backward_kernel,
        grid=(pairs,),
        out_shape=(low, low, low),
        in_specs=[
            whole((rows, width)),
            column_block(width, 0),
            column_block(rows, 0),
            column_block(rows, 0),
            column_block(rows, 0),
            whole((rows, LANES)),
            whole((rows, LANES)),
            whole((1, rows)),
            whole((rows, 1)),
            pl.BlockSpec((1, heads_each, rows), lambda pair: (pair, 0, 0)),
        ],
        out_specs=[column_block(rows, 0)] * 3,
        scratch_shapes=[
            pltpu.VMEM((rows, LANES), jnp.bfloat16),
            pltpu.VMEM((LANES, rows), jnp.bfloat16),
            pltpu.VMEM((rows, LANES), jnp.float32),
            pltpu.VMEM((rows, LANES), jnp.float32),
            pltpu.VMEM((rows, LANES), jnp.float32),
        ],
        compiler_params=pltpu.CompilerParams(vmem_limit_bytes=VMEM_LIMIT),
        cost_estimate=pl.CostEstimate(
            flops=2 * rows * width * width_here + 10 * rows * rows * width_here,
            bytes_accessed=2 * (rows * width + width * width_here + 7 * rows * width_here),
            transcendentals=rows * rows * width_here // HEAD_DIM,
        ),
    )(
        grad_rows, attn_pack, queries, key_rows, values, cosine, sine,
        starts[None, :], starts[:, None], lse,
    )


def shards(tokens, offsets, w_qkv, w_attn_out, w_in, w_mlp_out, gain_attn, gain_mlp, cotangent):
    rows_here = tokens.shape[0]
    group_rows = rows_here * lax.axis_size("tensor")
    model_here = w_qkv.shape[0]
    width_here = w_qkv.shape[2]
    hidden_here = w_in.shape[2]
    half_at = lax.axis_index("tensor") * rows_here
    position = (jnp.arange(group_rows, dtype=jnp.int32) + half_at) % group_rows
    starts = seq_starts(offsets[0], position)
    cosine_tab, sine_tab = rope_tables(position - starts)

    attn_pack, pending = gather_both(
        padded([w_qkv.reshape(model_here, 3 * width_here), gain_attn[:, None]]),
        padded(
            [w_attn_out.T, w_in.reshape(model_here, 2 * hidden_here), w_mlp_out.T, gain_mlp[:, None]]
        ),
    )
    gain_one = attn_pack[:, 3 * width_here].astype(jnp.float32)
    qkv_full = attn_pack[:, : 3 * width_here]

    token_rows = spread_rows(tokens)
    cotangent_rows = spread_rows(cotangent)
    grad_rows = cotangent_rows.astype(jnp.bfloat16)
    unit_one, scale_one = norm_parts(token_rows)
    normed_all = (unit_one * gain_one).astype(jnp.bfloat16)
    queries, key_rows, values, context, lse = attention_forward(
        normed_all, attn_pack, cosine_tab, sine_tab, starts, width_here
    )

    rest_pack = gather_rest(pending, lse)
    mlp_at = width_here
    mlp_end = width_here + 2 * hidden_here
    attn_out_full = rest_pack[:, :width_here]
    mlp_in_full = rest_pack[:, mlp_at:mlp_end]
    mlp_out_full = rest_pack[:, mlp_end : mlp_end + hidden_here]
    gain_two = rest_pack[:, mlp_end + hidden_here].astype(jnp.float32)
    attended = collect_all(dot_nt(context, attn_out_full), rows_here)
    hidden = token_rows + attended
    unit_two, scale_two = norm_parts(hidden)
    mlp_rows = (unit_two * gain_two).astype(jnp.bfloat16)
    gate_part = dot_nn(mlp_rows, mlp_in_full[:, :hidden_here])
    up_part = dot_nn(mlp_rows, mlp_in_full[:, hidden_here:])
    grad_product = dot_nn(grad_rows, mlp_out_full)
    bell = 0.5 * (1.0 + lax.erf(gate_part * math.sqrt(0.5)))
    activated = gate_part * bell
    slope = bell + gate_part * jnp.exp(-0.5 * gate_part * gate_part) * (1.0 / math.sqrt(2 * math.pi))
    product_rows = (activated * up_part).astype(jnp.bfloat16)
    grad_gate_up = jnp.concatenate(
        [
            (grad_product * up_part * slope).astype(jnp.bfloat16),
            (grad_product * activated).astype(jnp.bfloat16),
        ],
        axis=1,
    )
    grad_normed_two = collect_all(dot_nt(grad_gate_up, mlp_in_full), rows_here)
    grad_hidden = cotangent_rows + norm_backward(grad_normed_two, gain_two, unit_two, scale_two)
    grad_gain_two = jnp.sum((grad_normed_two * unit_two)[:rows_here], axis=0)
    grad_hidden_rows = grad_hidden.astype(jnp.bfloat16)
    grads_three = attention_backward(
        grad_hidden_rows, rest_pack, queries, key_rows, values,
        cosine_tab, sine_tab, starts, lse,
    )
    mlp_terms = padded(
        [
            dot_tn(mlp_rows, grad_gate_up).astype(jnp.bfloat16),
            dot_tn(grad_rows, product_rows).astype(jnp.bfloat16),
            two_terms(grad_gain_two),
        ]
    )
    mlp_sums = sum_blocks(mlp_terms, grads_three[0])
    branch = collect_own(dot_nt(product_rows, mlp_out_full), rows_here)
    outputs = hidden[:rows_here] + branch

    grad_projected = jnp.concatenate(grads_three, axis=1)
    grad_normed_one = collect_own(dot_nt(grad_projected, qkv_full), rows_here)
    grad_tokens = grad_hidden[:rows_here] + norm_backward(
        grad_normed_one, gain_one, unit_one[:rows_here], scale_one[:rows_here]
    )
    grad_gain_one = jnp.sum(grad_normed_one * unit_one[:rows_here], axis=0)
    attn_terms = padded(
        [
            dot_tn(normed_all, grad_projected).astype(jnp.bfloat16),
            dot_tn(grad_hidden_rows, context).astype(jnp.bfloat16),
            two_terms(grad_gain_one),
        ]
    )
    attn_sums = sum_blocks(attn_terms)

    gain_one_cols = attn_sums[:, 4 * width_here : 4 * width_here + 2].sum(axis=1)
    gain_two_cols = mlp_sums[:, 3 * hidden_here : 3 * hidden_here + 2].sum(axis=1)
    gains = jnp.stack([gain_one_cols, gain_two_cols])
    gains = gains + other_half(gains)
    return (
        outputs,
        grad_tokens,
        attn_sums[:, : 3 * width_here].reshape(model_here, 3, width_here),
        attn_sums[:, 3 * width_here : 4 * width_here].T,
        mlp_sums[:, : 2 * hidden_here].reshape(model_here, 2, hidden_here),
        mlp_sums[:, 2 * hidden_here : 3 * hidden_here].T,
        gains[0],
        gains[1],
    )


def fast_columns(width_here, hidden_here):
    main = hidden_here // LANES * LANES
    pairs = width_here // LANES
    at = {"gains": (0, LANES)}
    place = LANES
    for pair in range(pairs):
        at["pair%d" % pair] = (place, 3 * LANES)
        place += 3 * LANES
    for name, size in (
        ("out", width_here), ("mlp", main + LANES), ("gate", main), ("up", main), ("tail", LANES),
    ):
        at[name] = (place, size)
        place += size
    at["total"] = (0, place)
    return at


def pack_shards(w_qkv, w_attn_out, w_in, w_mlp_out, gain_attn, gain_mlp):
    height, _, width_here = w_qkv.shape
    hidden_here = w_in.shape[2]
    main = hidden_here // LANES * LANES
    pairs = width_here // LANES
    gains = jnp.concatenate(
        [gain_attn[:, None], gain_mlp[:, None], jnp.zeros((height, LANES - 2), jnp.bfloat16)], axis=1
    )
    by_pair = w_qkv.reshape(height, 3, pairs, LANES).transpose(0, 2, 1, 3)
    short = main + LANES - hidden_here
    return jnp.concatenate(
        [
            gains,
            by_pair.reshape(height, 3 * width_here),
            w_attn_out.T,
            w_mlp_out.T,
            jnp.zeros((height, short), jnp.bfloat16),
            w_in[:, 0, :main],
            w_in[:, 1, :main],
            w_in[:, 0, main:],
            w_in[:, 1, main:],
        ],
        axis=1,
    )


class Links:
    def __init__(self, ref):
        self.ref = ref
        self.dp = lax.axis_index("dp")
        self.core = lax.axis_index("tensor")
        self.x = self.dp % 2
        self.y = (self.dp // 2) % 2
        self.z = self.dp // 4
        plane = self.dp % 4
        self.x_side = self.dp + 1 - 2 * self.x
        self.y_side = self.dp + 2 - 4 * self.y
        self.z_of = [None, self.z + 1 - 2 * (self.z % 2), (self.z + 2) % 4, 3 - self.z]
        self.z_side = [None] + [place * 4 + plane for place in self.z_of[1:]]
        self.started = []

    def enter(self):
        barrier = pltpu.get_barrier_semaphore()
        others = [(self.x_side, self.core), (self.y_side, self.core), (self.dp, 1 - self.core)]
        others += [(place, self.core) for place in self.z_side[1:]]
        for other in others:
            pl.semaphore_signal(
                barrier, inc=1, device_id=other, device_id_type=pl.DeviceIdType.MESH
            )
        pl.semaphore_wait(barrier, len(others))

    def copy(self, source, target, sems, place, device):
        return pltpu.make_async_remote_copy(
            src_ref=source,
            dst_ref=target,
            send_sem=sems[0].at[place],
            recv_sem=sems[1].at[place],
            device_id=device,
            device_id_type=pl.DeviceIdType.MESH,
        )

    def start(self, *copies):
        for copy in copies:
            copy.start()
            self.started.append(copy)

    def to_core(self, source, target, place):
        copy = self.copy(
            source, target, (self.ref.core_out, self.ref.core_in), place, (self.dp, 1 - self.core)
        )
        self.start(copy)
        return copy

    def finish(self):
        for copy in self.started:
            copy.wait_send()


class Gather(Links):
    def __init__(self, ref, chunks):
        super().__init__(ref)
        self.chunks = chunks
        self.got = {}

    def send_z(self, name):
        chunk = list(self.chunks).index(name)
        cols = pl.ds(*self.chunks[name])
        block = self.ref.full.at[self.z, self.y, self.x, :, cols]
        copies = [
            self.copy(
                block, block, (self.ref.far_out, self.ref.far_in), 3 * chunk + step - 1,
                (self.z_side[step], self.core),
            )
            for step in (1, 2, 3)
        ]
        self.start(*copies)
        self.got[name] = copies

    def arrive(self, name):
        for copy in self.got[name]:
            copy.wait_recv()

    def near(self, name, stage, first, second):
        chunk = list(self.chunks).index(name)
        sems = (self.ref.near_out, self.ref.near_in)
        place = 4 * chunk + 2 * stage
        copies = [
            self.copy(first[0], first[0], sems, place, (first[1], self.core)),
            self.copy(second[0], second[0], sems, place + 1, (second[1], self.core)),
        ]
        self.arrive(name)
        self.start(*copies)
        self.got[name] = copies

    def send_one(self, name):
        cols = pl.ds(*self.chunks[name])
        low, high = pl.ds(0, 2), pl.ds(2, 2)
        full = self.ref.full
        self.near(
            name, 0,
            (full.at[low, self.y, self.x, :, cols], self.x_side),
            (full.at[high, self.y, self.x, :, cols], self.y_side),
        )

    def send_two(self, name):
        cols = pl.ds(*self.chunks[name])
        low, high = pl.ds(0, 2), pl.ds(2, 2)
        both = pl.ds(0, 2)
        full = self.ref.full
        self.near(
            name, 1,
            (full.at[low, self.y, both, :, cols], self.y_side),
            (full.at[high, both, self.x, :, cols], self.x_side),
        )


def weights_at(full, span):
    block = full[:, :, :, :, span[0] : span[0] + span[1]]
    return block.reshape(-1, span[1])


def row_loop(rows, block):
    def wrap(body):
        @pl.loop(0, rows // block)
        def _(step):
            body(pl.ds(pl.multiple_of(step * block, block), block))

    return wrap


def front_kernel(names, spans, *refs):
    ref = types.SimpleNamespace(**dict(zip(names, refs)))
    half, width = ref.tok.shape
    rows = 2 * half
    pairs = (spans["out"][1]) // LANES
    main = spans["gate"][1]
    chunk_names = ["gains"] + ["pair%d" % pair for pair in range(pairs)] + ["out", "mlp"]
    chunks = {name: spans[name] for name in chunk_names}
    chunks["gate"] = spans["gate"]
    chunks["up"] = (spans["up"][0], main + LANES)
    link = Gather(ref, chunks)
    core = link.core
    own = pl.ds(pl.multiple_of(core * half, half), half)
    own_at = core * half
    other_at = (1 - core) * half
    part = 256

    link.enter()
    ref.full[link.z, link.y, link.x] = ref.pack[...]
    link.send_z("gains")
    link.send_z("pair0")
    link.send_z("pair1")

    @row_loop(half, 128)
    def _(at):
        unit, scale = norm_parts(ref.tok[at, :])
        ref.unit_one[at, :] = unit
        ref.scale_one[at, :] = jnp.broadcast_to(scale, (128, LANES))
        here = pl.ds(pl.multiple_of(own_at + at.start, 128), 128)
        ref.grad_rows[here, :] = ref.cot[at, :].astype(jnp.bfloat16)

    got_grad = link.to_core(ref.grad_rows.at[own, :], ref.grad_rows.at[own, :], 0)
    link.send_one("gains")

    shift = jnp.int32(0)
    for slot in range(ref.offsets.shape[1]):
        entry = ref.offsets[0, slot]
        shift = jnp.maximum(shift, jnp.where(entry <= half - 1, entry, 0))

    def source_of(place):
        moved = place + shift
        return jnp.where(moved >= rows, moved - rows, moved)

    def start_of(place):
        start = jnp.zeros_like(place)
        for slot in range(ref.offsets.shape[1]):
            entry = ref.offsets[0, slot]
            start = jnp.maximum(start, jnp.where(place >= entry, entry, 0))
        return start

    @row_loop(rows, part)
    def _(at):
        place = source_of(lax.broadcasted_iota(jnp.int32, (part, LANES), 0) + at.start)
        start = start_of(place)
        angle = (place - start).astype(jnp.float32) * ref.inverse[...]
        lane = lax.broadcasted_iota(jnp.int32, (part, LANES), 1)
        sine = jnp.sin(angle)
        ref.cosine[at, :] = jnp.cos(angle)
        ref.sine[at, :] = jnp.where(lane % HEAD_DIM < HEAD_DIM // 2, -sine, sine)

    link.send_two("gains")
    link.send_z("pair2")
    key_start = start_of(source_of(lax.broadcasted_iota(jnp.int32, (half, 1), 0) + half))
    query_start = start_of(source_of(lax.broadcasted_iota(jnp.int32, (1, half), 1) + half))
    ref.bias[...] = jnp.where(key_start == query_start, 0.0, NEGATIVE)

    @row_loop(rows, part)
    def _(at):
        down = lax.broadcasted_iota(jnp.int32, (part, rows), 0) + at.start
        along = lax.broadcasted_iota(jnp.int32, (part, rows), 1)
        ref.perm[at, :] = jnp.where(source_of(down) == along, 1.0, 0.0).astype(jnp.bfloat16)
        ref.perm_back[at, :] = jnp.where(source_of(along) == down, 1.0, 0.0).astype(jnp.bfloat16)

    link.send_one("pair0")
    link.arrive("gains")
    slot = lax.broadcasted_iota(jnp.int32, (8, LANES), 0)
    lane = lax.broadcasted_iota(jnp.int32, (8, LANES), 1)
    pick = jnp.where(slot == lane, 1.0, 0.0).astype(jnp.bfloat16)
    ref.gain[...] = dot_nt(pick, weights_at(ref.full, spans["gains"]))

    @row_loop(half, 128)
    def _(at):
        here = pl.ds(pl.multiple_of(own_at + at.start, 128), 128)
        ref.normed[here, :] = (ref.unit_one[at, :] * ref.gain[0:1, :]).astype(jnp.bfloat16)

    got_normed = link.to_core(ref.normed.at[own, :], ref.normed.at[own, :], 1)
    link.send_one("pair1")
    link.send_two("pair0")
    link.send_z("out")
    got_normed.wait_recv()

    @row_loop(rows, part)
    def _(at):
        ref.rolled[at, :] = dot_nn(ref.perm[at, :], ref.normed[...]).astype(jnp.bfloat16)

    link.send_one("pair2")
    link.send_two("pair1")
    link.send_z("mlp")

    def project(pair):
        link.arrive("pair%d" % pair)
        cols = slice(pair * LANES, (pair + 1) * LANES)

        @row_loop(rows, part)
        def _(at):
            three = dot_nn(ref.rolled[at, :], weights_at(ref.full, spans["pair%d" % pair]))
            lane = lax.broadcasted_iota(jnp.int32, (part, LANES), 1)
            cosine, sine = ref.cosine[at, :], ref.sine[at, :]
            query = turn(three[:, :LANES], cosine, sine, lane) * SCALE
            ref.queries[at, cols] = query.astype(jnp.bfloat16)
            ref.keys[at, cols] = turn(
                three[:, LANES : 2 * LANES], cosine, sine, lane
            ).astype(jnp.bfloat16)
            ref.values[at, cols] = three[:, 2 * LANES :].astype(jnp.bfloat16)
            ref.values_t[:, at] = three[:, 2 * LANES :].T.astype(jnp.bfloat16)

    def attend(pair, first):
        cols = slice(pair * LANES, (pair + 1) * LANES)
        base = 0 if first else half

        @pl.loop(0, half // part)
        def _(step):
            at = pl.ds(pl.multiple_of(base + step * part, part), part)
            query_pair = ref.queries[at, cols]
            lane = lax.broadcasted_iota(jnp.int32, (part, LANES), 1)
            parts = []
            for head in range(LANES // HEAD_DIM):
                query = jnp.where(lane // HEAD_DIM == head, query_pair, 0)
                scores = dot_nt(ref.keys[base : base + half, cols], query)
                if not first:
                    scores = scores + ref.bias[:, pl.ds(pl.multiple_of(step * part, part), part)]
                top = jnp.max(scores, axis=0, keepdims=True)
                terms = jnp.exp(scores - top)
                total = jnp.sum(terms, axis=0, keepdims=True)
                mixed = dot_nn(
                    ref.values_t[head * HEAD_DIM : (head + 1) * HEAD_DIM, base : base + half],
                    terms.astype(jnp.bfloat16),
                )
                parts.append(mixed * (1.0 / total))
                ref.lse[pair, head : head + 1, at] = top + jnp.log(total)
            ref.context_rolled[at, cols] = jnp.concatenate(parts, axis=0).T.astype(jnp.bfloat16)

    project(0)
    attend(0, True)
    link.send_one("out")
    link.send_two("pair2")
    link.send_z("gate")
    attend(0, False)
    project(1)
    attend(1, True)
    link.send_one("mlp")
    link.send_two("out")
    link.send_z("up")
    attend(1, False)
    project(2)
    attend(2, True)
    link.send_one("gate")
    link.send_two("mlp")
    attend(2, False)

    @row_loop(rows, part)
    def _(at):
        ref.context[at, :] = dot_nn(ref.perm_back[at, :], ref.context_rolled[...]).astype(jnp.bfloat16)

    link.send_one("up")
    link.send_two("gate")
    link.arrive("out")

    def pair_sum(product, place, keep):
        @row_loop(half, part)
        def _(at):
            there = pl.ds(pl.multiple_of(other_at + at.start, part), part)
            ref.sent[place, at, :] = product(there).astype(jnp.bfloat16)

        got = link.to_core(ref.sent.at[place], ref.taken.at[place], 2 + place)

        @row_loop(half, part)
        def _(at):
            here = pl.ds(pl.multiple_of(own_at + at.start, part), part)
            keep[at, :] = product(here)

        return got

    got_attended = pair_sum(
        lambda at: dot_nt(ref.context[at, :], weights_at(ref.full, spans["out"])), 0, ref.hidden
    )
    got_attended.wait_recv()

    @row_loop(half, 128)
    def _(at):
        hidden = ref.tok[at, :] + ref.hidden[at, :] + ref.taken[0, at, :].astype(jnp.float32)
        ref.hidden[at, :] = hidden
        unit, scale = norm_parts(hidden)
        ref.unit_two[at, :] = unit
        ref.scale_two[at, :] = jnp.broadcast_to(scale, (128, LANES))
        here = pl.ds(pl.multiple_of(own_at + at.start, 128), 128)
        ref.normed_mlp[here, :] = (unit * ref.gain[1:2, :]).astype(jnp.bfloat16)

    got_mlp = link.to_core(ref.normed_mlp.at[own, :], ref.normed_mlp.at[own, :], 6)
    link.send_two("up")
    got_grad.wait_recv()
    link.arrive("mlp")

    @row_loop(rows, part)
    def _(at):
        ref.grad_product[at, :] = dot_nn(ref.grad_rows[at, :], weights_at(ref.full, spans["mlp"]))

    got_mlp.wait_recv()
    link.arrive("gate")
    link.arrive("up")

    def gated(gate, up, grad):
        bell = 0.5 * (1.0 + lax.erf(gate * math.sqrt(0.5)))
        activated = gate * bell
        slope = bell + gate * jnp.exp(-0.5 * gate * gate) * (1.0 / math.sqrt(2 * math.pi))
        return activated * up, grad * up * slope, grad * activated

    @row_loop(rows, part)
    def _(at):
        low = ref.normed_mlp[at, :]
        gate = dot_nn(low, weights_at(ref.full, spans["gate"]))
        up = dot_nn(low, weights_at(ref.full, spans["up"]))
        product, grad_gate, grad_up = gated(gate, up, ref.grad_product[at, :main])
        ref.product[at, :main] = product.astype(jnp.bfloat16)
        ref.grad_gate_up[at, :main] = grad_gate.astype(jnp.bfloat16)
        ref.grad_gate_up[at, main : 2 * main] = grad_up.astype(jnp.bfloat16)
        tail = dot_nn(low, weights_at(ref.full, spans["tail"]))
        product, grad_gate, grad_up = gated(
            tail, pltpu.roll(tail, LANES // 2, axis=1), ref.grad_product[at, main:]
        )
        lane = lax.broadcasted_iota(jnp.int32, (part, LANES), 1)
        lower = lane < LANES // 2
        ref.product[at, main:] = jnp.where(lower, product, 0.0).astype(jnp.bfloat16)
        ref.grad_gate_up[at, 2 * main :] = jnp.where(
            lower, grad_gate, pltpu.roll(grad_up, LANES // 2, axis=1)
        ).astype(jnp.bfloat16)

    inner = (spans["gate"][0], 2 * main + LANES)
    got_normed_two = pair_sum(
        lambda at: dot_nt(ref.grad_gate_up[at, :], weights_at(ref.full, inner)), 1, ref.grad_hidden
    )
    got_branch = pair_sum(
        lambda at: dot_nt(ref.product[at, :], weights_at(ref.full, spans["mlp"])), 2, ref.outputs
    )
    got_normed_two.wait_recv()
    ref.gain_rows[...] = jnp.zeros_like(ref.gain_rows)

    @row_loop(half, 128)
    def _(at):
        incoming = ref.grad_hidden[at, :] + ref.taken[1, at, :].astype(jnp.float32)
        unit = ref.unit_two[at, :]
        ref.gain_rows[1:2, :] += jnp.sum(incoming * unit, axis=0, keepdims=True)
        grad = ref.cot[at, :] + norm_backward(
            incoming, ref.gain[1:2, :], unit, ref.scale_two[at, 0:1]
        )
        ref.grad_hidden[at, :] = grad
        here = pl.ds(pl.multiple_of(own_at + at.start, 128), 128)
        ref.grad_low[here, :] = grad.astype(jnp.bfloat16)

    got_low = link.to_core(ref.grad_low.at[own, :], ref.grad_low.at[own, :], 7)
    got_branch.wait_recv()

    @row_loop(half, 128)
    def _(at):
        ref.outputs[at, :] = (
            ref.outputs[at, :] + ref.hidden[at, :] + ref.taken[2, at, :].astype(jnp.float32)
        )

    got_low.wait_recv()
    ref.weights[...] = weights_at(ref.full, spans["total"])
    link.finish()


def call_front(pack, tokens, cotangent, offsets, spans):
    half, width = tokens.shape
    rows = 2 * half
    height, total = pack.shape
    width_here = spans["out"][1]
    pairs = width_here // LANES
    main = spans["gate"][1]
    half_dim = HEAD_DIM // 2
    inverse = jnp.power(
        jnp.float32(ROPE_BASE), -2.0 * jnp.arange(half_dim, dtype=jnp.float32) / HEAD_DIM
    )
    inverse = jnp.tile(inverse, LANES // half_dim)[None, :]
    low, wide = jnp.bfloat16, jnp.float32
    outs = dict(
        outputs=((half, width), wide),
        grad_hidden=((half, width), wide),
        gain_rows=((8, width), wide),
        gain=((8, width), wide),
        unit_one=((half, width), wide),
        scale_one=((half, LANES), wide),
        cosine=((rows, LANES), wide),
        sine=((rows, LANES), wide),
        lse=((pairs, LANES // HEAD_DIM, rows), wide),
        rolled=((rows, width), low),
        queries=((rows, width_here), low),
        keys=((rows, width_here), low),
        values=((rows, width_here), low),
        context=((rows, width_here), low),
        grad_rows=((rows, width), low),
        normed_mlp=((rows, width), low),
        product=((rows, main + LANES), low),
        grad_gate_up=((rows, 2 * main + LANES), low),
        grad_low=((rows, width), low),
        weights=((width, total), low),
    )
    chunk_count = 1 + pairs + 4
    scratch = dict(
        full=pltpu.VMEM((4, 2, 2, height, total), low),
        normed=pltpu.VMEM((rows, width), low),
        perm=pltpu.VMEM((rows, rows), low),
        perm_back=pltpu.VMEM((rows, rows), low),
        bias=pltpu.VMEM((half, half), wide),
        values_t=pltpu.VMEM((LANES, rows), low),
        context_rolled=pltpu.VMEM((rows, width_here), low),
        sent=pltpu.VMEM((3, half, width), low),
        taken=pltpu.VMEM((3, half, width), low),
        hidden=pltpu.VMEM((half, width), wide),
        unit_two=pltpu.VMEM((half, width), wide),
        scale_two=pltpu.VMEM((half, LANES), wide),
        grad_product=pltpu.VMEM((rows, main + LANES), wide),
        far_out=pltpu.SemaphoreType.DMA((3 * chunk_count,)),
        far_in=pltpu.SemaphoreType.DMA((3 * chunk_count,)),
        near_out=pltpu.SemaphoreType.DMA((4 * chunk_count,)),
        near_in=pltpu.SemaphoreType.DMA((4 * chunk_count,)),
        core_out=pltpu.SemaphoreType.DMA((8,)),
        core_in=pltpu.SemaphoreType.DMA((8,)),
    )
    names = ["offsets", "pack", "tok", "cot", "inverse"] + list(outs) + list(scratch)
    vmem = pl.BlockSpec(memory_space=pltpu.VMEM)
    results = pl.pallas_call(
        functools.partial(front_kernel, names, spans),
        out_shape=[jax.ShapeDtypeStruct(*entry) for entry in outs.values()],
        in_specs=[pl.BlockSpec(memory_space=pltpu.SMEM)] + [vmem] * 4,
        out_specs=[vmem] * len(outs),
        scratch_shapes=list(scratch.values()),
        compiler_params=pltpu.CompilerParams(
            collective_id=0, has_side_effects=True, vmem_limit_bytes=60 * 1024 * 1024
        ),
        cost_estimate=pl.CostEstimate(
            flops=12 * 10**9, bytes_accessed=30 * 10**6, transcendentals=10**7
        ),
    )(offsets, pack, tokens, cotangent, inverse)
    return types.SimpleNamespace(**dict(zip(outs, results)))


def fast_shards(tokens, offsets, w_qkv, w_attn_out, w_in, w_mlp_out, gain_attn, gain_mlp, cotangent):
    half = tokens.shape[0]
    rows = 2 * half
    height, _, width_here = w_qkv.shape
    hidden_here = w_in.shape[2]
    pairs = width_here // LANES
    main = hidden_here // LANES * LANES
    spans = fast_columns(width_here, hidden_here)
    pack = pack_shards(w_qkv, w_attn_out, w_in, w_mlp_out, gain_attn, gain_mlp)
    f = call_front(pack, tokens, cotangent, offsets, spans)
    core = lax.axis_index("tensor")
    shift = seq_starts(offsets[0], jnp.full((1,), half - 1, jnp.int32))[0]
    place = (jnp.arange(rows, dtype=jnp.int32) + shift) % rows
    starts = seq_starts(offsets[0], place)
    pick = lambda name: f.weights[:, spans[name][0] : spans[name][0] + spans[name][1]]
    grads_three = attention_backward(
        jnp.roll(f.grad_low, -shift, axis=0), pick("out"), f.queries * 8, f.keys, f.values,
        f.cosine, f.sine, starts, f.lse,
    )
    grad_projected = jnp.concatenate(
        [g[:, p * LANES : (p + 1) * LANES] for p in range(pairs) for g in grads_three], axis=1
    )
    at = spans["pair0"][0]
    qkv_full = f.weights[:, at : at + 3 * width_here]
    mlp_terms = padded(
        [
            dot_tn(f.normed_mlp, f.grad_gate_up).astype(jnp.bfloat16),
            dot_tn(f.grad_rows, f.product[:, :hidden_here]).astype(jnp.bfloat16),
            two_terms(f.gain_rows[1]),
        ]
    )
    mlp_sums = sum_blocks(mlp_terms)
    partial_one = dot_nt(jnp.roll(grad_projected, shift, axis=0), qkv_full)
    mine = lax.dynamic_slice_in_dim(partial_one, core * half, half, 0)
    other = lax.dynamic_slice_in_dim(partial_one, (1 - core) * half, half, 0)
    grad_normed_one = mine + other_half(other.astype(jnp.bfloat16)).astype(jnp.float32)
    grad_tokens = f.grad_hidden + norm_backward(
        grad_normed_one, f.gain[0:1], f.unit_one, f.scale_one[:, 0:1]
    )
    attn_terms = padded(
        [
            dot_tn(f.rolled, grad_projected).astype(jnp.bfloat16),
            dot_tn(f.grad_low, f.context).astype(jnp.bfloat16),
            two_terms(jnp.sum(grad_normed_one * f.unit_one, axis=0)),
        ]
    )
    attn_sums = sum_blocks(attn_terms)
    gain_one_cols = attn_sums[:, 4 * width_here : 4 * width_here + 2].sum(axis=1)
    gain_two_cols = mlp_sums[:, 3 * hidden_here : 3 * hidden_here + 2].sum(axis=1)
    gains = jnp.stack([gain_one_cols, gain_two_cols])
    gains = gains + other_half(gains)
    tail = mlp_sums[:, 2 * main : 2 * hidden_here]
    grad_in = jnp.stack(
        [
            jnp.concatenate([mlp_sums[:, :main], tail[:, : hidden_here - main]], axis=1),
            jnp.concatenate([mlp_sums[:, main : 2 * main], tail[:, hidden_here - main :]], axis=1),
        ],
        axis=1,
    )
    return (
        f.outputs,
        grad_tokens,
        attn_sums[:, : 3 * width_here]
        .reshape(height, pairs, 3, LANES)
        .transpose(0, 2, 1, 3)
        .reshape(height, 3, width_here),
        attn_sums[:, 3 * width_here : 4 * width_here].T,
        grad_in,
        mlp_sums[:, 2 * hidden_here : 3 * hidden_here].T,
        gains[0],
        gains[1],
    )


def solution(mesh):
    in_specs = (
        P(("dp", "tensor"), None),
        P("dp", None),
        P("dp", None, "tensor"),
        P("tensor", "dp"),
        P("dp", None, "tensor"),
        P("tensor", "dp"),
        P("dp"),
        P("dp"),
        P(("dp", "tensor"), None),
    )
    out_specs = (
        P(("dp", "tensor"), None),
        P(("dp", "tensor"), None),
        P("dp", None, "tensor"),
        P("tensor", "dp"),
        P("dp", None, "tensor"),
        P("tensor", "dp"),
        P("dp"),
        P("dp"),
    )
    sizes = dict(mesh.shape)
    body = fast_shards if (sizes["dp"], sizes["tensor"]) == (16, 2) else shards
    return jax.shard_map(body, mesh=mesh, in_specs=in_specs, out_specs=out_specs, check_vma=False)
```

profile of v0, /device:TPU:0, one launch (start us, length us, event | category | flops | bytes accessed | tf_op | source)
XLA Modules:
  0.0 243.1 jit_solution(9214620305259058527)
XLA Ops:
  0.7 1.1 fusion.25
  1.8 0.9 fusion.24
  2.7 0.9 reshape.170
  3.9 0.8 copy.84
  4.6 0.8 copy.85
  6.1 0.8 concatenate.36.refs_1_
  6.9 82.0 %shard_map.152 = (f32[512,768]{1,0:T(8,128)}, f32[512,768]{1,0:T(8,128)}, f32[8,768]{1,0:T(8,128)}, f32[8,768]{1,0:T(8,128)}, f32[512,768]{1,0:T(8,128)}, /*inde...) custom-call(s32[1,16]{1,0:T(1,128)} %refs_0_.1, ...), custom_call_target="tpu_custom_call" | custom-call | flops 12000000000 | bytes 30000000 | tf_op jit(solution)/shard_map/pallas_call | solution.py:952
  89.7 4.4 %convolution_convert_fusion = bf16[768,1152]{1,0:T(8,128)(2,1)S(1)} fusion(bf16[1024,768]{1,0:T(8,128)(2,1)} %get-tuple-element.49, bf16[1024,1152]{1,0:T(8,128)(2,1)} %get-tuple-element.50), kind=kOutput, calls=%fused_computation.2 | convolution fusion | flops 1812824064 | bytes 5701632 | tf_op jit(solution)/shard_map/dot_general | solution.py:180
  94.1 1.4 copy.98
  96.6 1.2 convolution_convert_fusion.2
  98.4 1.0 copy.99
  99.9 3.6 %concatenate.45 = bf16[4,4,48,1792]{3,2,0,1:T(8,128)(2,1)S(1)} concatenate(bf16[4,4,48,1152]{3,2,0,1:T(8,128)(2,1)} %copy.98, bf16[4,4,48,576]{3,2,0,1:T(8,128)(2,1)} %copy.99, bf16[4,4,48,1]{3,2,0,1:T(8,128)(2,1)S(1)} %copy.100, bf16[4,4,48,1]{3,2,0,1:T(8,128)(2,1)S(1)} %copy.101, bf16[4,4,48,62]{3,2,0,1:T(8,128)(2,1)S(1)} %broadcast_in_dim.50), dimensions={3} | concatenate | bytes 5505024 | tf_op jit(solution)/shard_map/concatenate | solution.py:166
  103.5 1.4 dynamic-slice_bitcast_fusion.2
  104.9 0.8 copy-done.4
  105.7 1.1 collective-permute-start.7
  106.8 0.9 collective-permute-start.8
  107.7 1.5 collective-permute-start.9
  113.1 1.1 slice.98.wo_ref
  114.7 4.2 %fusion.4.grad_ref = bf16[1024,768]{1,0:T(8,128)(2,1)} fusion(s32[]{:T(128)S(6)} %select_n.106, bf16[1024,768]{1,0:T(8,128)(2,1)} %get-tuple-element.34), kind=kLoop, calls=%fused_computation.9 | loop fusion | flops 3145728 | bytes 3145732 | tf_op jit(solution)/shard_map/jit(_roll_dynamic)/concatenate | solution.py:984
  118.9 33.7 %shard_map.153 = (bf16[1024,384]{1,0:T(8,128)(2,1)S(1)}, bf16[1024,384]{1,0:T(8,128)(2,1)S(1)}, bf16[1024,384]{1,0:T(8,128)(2,1)S(1)}) custom-call(bf16[1024,768]{1,0:T(8,128)(2,1)} %fusion.4.grad_ref, bf16[768,384]{1,0:T(8,128)(2,1)S(1)} %slice.98.wo_ref, bf16[1024,384]{1,0:T(8,128)(2,1)S(1)} %broadcast_multiply_fusion.q_ref, ...), custom_call_target="tpu_custom_call" | custom-call | flops 4630511616 | bytes 7667712 | tf_op jit(solution)/shard_map/pallas_call | solution.py:313
  157.8 0.8 slice_dynamic-update-slice_fusion.1
  158.6 0.8 slice_dynamic-update-slice_fusion
  159.4 5.4 %fusion.1 = f32[1024,768]{1,0:T(8,128)S(1)} fusion(s32[]{:T(128)S(6)} %select_n.110, bf16[1024,1152]{1,0:T(8,128)(2,1)} %slice_dynamic-update-slice_fusion, bf16[768,3456]{1,0:T(8,128)(2,1)} %get-tuple-element.35), kind=kOutput, calls=%fused_computation.7 | convolution fusion | flops 1816657920 | bytes 7274500 | tf_op jit(solution)/shard_map/dot_general | solution.py:174
  164.8 1.1 dynamic-slice_convert_fusion
  165.9 3.7 %convolution_convert_fusion.3 = bf16[768,384]{1,0:T(8,128)(2,1)} fusion(bf16[1024,768]{1,0:T(8,128)(2,1)} %get-tuple-element.34, bf16[1024,384]{1,0:T(8,128)(2,1)} %get-tuple-element.48), kind=kOutput, calls=%fused_computation.21 | convolution fusion | flops 604274688 | bytes 2949120 | tf_op jit(solution)/shard_map/dot_general | solution.py:180
  169.8 5.2 %convolution_convert_fusion.1 = bf16[768,1152]{1,0:T(8,128)(2,1)} fusion(bf16[1024,768]{1,0:T(8,128)(2,1)S(1)} %copy-done.19, bf16[1024,1152]{1,0:T(8,128)(2,1)} %slice_dynamic-update-slice_fusion), kind=kOutput, calls=%fused_computation.3 | convolution fusion | flops 1812824064 | bytes 5701632 | tf_op jit(solution)/shard_map/dot_general | solution.py:180
  175.8 3.0 %copy.89 = bf16[4,4,48,1152]{3,2,0,1:T(8,128)(2,1)} copy(bf16[4,4,48,1152]{3,2,1,0:T(8,128)(2,1)} %bitcast.76) | data formatting | bytes 3538944 | tf_op jit(solution)/shard_map/concatenate | solution.py:166
  178.7 0.9 copy.90
  179.7 2.2 fusion.7
  181.9 0.8 copy-done.8
  182.7 0.8 constant_dynamic-slice_fusion.2
  183.5 1.2 collective-permute-start.10
  184.7 2.6 %collective-permute-start.11 = (bf16[1,48,1792]{2,1,0:T(8,128)(2,1)}, bf16[1,48,1792]{2,1,0:T(8,128)(2,1)S(1)}, u32[]{:S(2)}, u32[]{:S(2)}) collective-permute-start(bf16[1,48,1792]{2,1,0:T(8,128)(2,1)} %get-tuple-element.97), channel_id=1, source_target_pairs={{0,16},{2,18},{4,20},{6,22},{8,24},{10,26},{12,28},{14,30},{16,0},... | collective-permute-start | bytes 516104 | tf_op jit(solution)/shard_map/ppermute | solution.py:108
  187.9 1.8 multiply_reduce_fusion
  190.2 3.5 %concatenate.42 = bf16[4,4,48,1664]{3,2,0,1:T(8,128)(2,1)S(1)} concatenate(bf16[4,4,48,1152]{3,2,0,1:T(8,128)(2,1)} %copy.89, bf16[4,4,48,384]{3,2,0,1:T(8,128)(2,1)} %copy.90, bf16[4,4,48,1]{3,2,0,1:T(8,128)(2,1)S(1)} %copy.91, bf16[4,4,48,1]{3,2,0,1:T(8,128)(2,1)S(1)} %copy.92, bf16[4,4,48,126]{3,2,0,1:T(8,128)(2,1)S(1)} %broadcast_in_dim.49), dimensions={3} | concatenate | bytes 5111808 | tf_op jit(solution)/shard_map/concatenate | solution.py:166
  193.9 1.2 collective-permute-start.1
  195.1 0.9 collective-permute-start.2
  196.0 3.3 %multiply_add_fusion = f32[512,768]{1,0:T(8,128)} fusion(f32[512,768]{1,0:T(8,128)S(1)} %copy-done.9, f32[512,768]{1,0:T(8,128)S(1)} %copy-done.6, f32[512]{0:T(512)S(1)} %broadcast_multiply_fusion.1, f32[512]{0:T(512)S(1)} %broadcast_multiply_fusion.2, f32[768]{0:T(1024)S(1)} %slice_reduce_fusion.4, f32[512]{0:T(512)S(1)} %slice_reduce_fusion, ...), kind=kLoop, calls=%fused_computation.11 | loop fusion | flops 3145728 | bytes 7087108 | tf_op jit(solution)/shard_map/add | solution.py:1004
  199.3 1.5 collective-permute-start.3
  200.8 1.1 add_bitcast_fusion
  202.7 8.6 %collective-permute-done.1 = bf16[4,48,1664]{2,1,0:T(8,128)(2,1)S(1)} collective-permute-done((bf16[4,48,1664]{2,1,0:T(8,128)(2,1)S(1)}, bf16[4,48,1664]{2,1,0:T(8,128)(2,1)S(1)}, u32[]{:S(2)}, u32[]{:S(2)}) %collective-permute-start.1) | collective-permute-done | bytes 639008 | tf_op jit(solution)/shard_map/ppermute | solution.py:108
  211.3 13.0 %collective-permute-done.2 = bf16[4,48,1664]{2,1,0:T(8,128)(2,1)S(1)} collective-permute-done((bf16[4,48,1664]{2,1,0:T(8,128)(2,1)S(1)}, bf16[4,48,1664]{2,1,0:T(8,128)(2,1)S(1)}, u32[]{:S(2)}, u32[]{:S(2)}) %collective-permute-start.2) | collective-permute-done | bytes 639008 | tf_op jit(solution)/shard_map/ppermute | solution.py:108
  225.1 3.5 %collective-permute-start.5 = (bf16[1,48,1664]{2,1,0:T(8,128)(2,1)S(1)}, bf16[1,48,1664]{2,1,0:T(8,128)(2,1)S(1)}, u32[]{:S(2)}, u32[]{:S(2)}) collective-permute-start(bf16[1,48,1664]{2,1,0:T(8,128)(2,1)S(1)} %get-tuple-element.100), channel_id=1, source_target_pairs={{0,16},{2,18},{4,20},{6,22},{8,24},{10,26},{12,28},{14,30},{16,0},... | collective-permute-start | bytes 479240 | tf_op jit(solution)/shard_map/ppermute | solution.py:108
  229.2 0.8 copy.102
  230.2 0.9 collective-permute-done.4
  231.1 8.3 %collective-permute-done.5 = bf16[1,48,1664]{2,1,0:T(8,128)(2,1)S(1)} collective-permute-done((bf16[1,48,1664]{2,1,0:T(8,128)(2,1)S(1)}, bf16[1,48,1664]{2,1,0:T(8,128)(2,1)S(1)}, u32[]{:S(2)}, u32[]{:S(2)}) %collective-permute-start.5) | collective-permute-done | bytes 159776 | tf_op jit(solution)/shard_map/ppermute | solution.py:108
  240.6 0.8 reshape.174
  242.0 1.1 copy.121
  (110 shorter events, 17.0 us)
Async XLA Ops:
  0.6 5.4 %copy-start.15 = (bf16[384,48]{0,1:T(8,128)(2,1)S(1)}, bf16[384,48]{0,1:T(8,128)(2,1)}, u32[]{:S(2)}) copy-start(bf16[384,48]{0,1:T(8,128)(2,1)} %param.12) | copy-start | bytes 110596
  0.6 5.4 %copy-start.14 = (bf16[576,48]{0,1:T(8,128)(2,1)S(1)}, bf16[576,48]{0,1:T(8,128)(2,1)}, u32[]{:S(2)}) copy-start(bf16[576,48]{0,1:T(8,128)(2,1)} %param.14) | copy-start | bytes 165892
  94.1 2.0 copy-start.17
  94.1 2.4 copy-start.18
  103.5 2.2 copy-start.4
  103.5 5.7 %copy-start.16 = (s32[1,16]{1,0:T(1,128)S(1)}, s32[1,16]{1,0:T(1,128)}, u32[]{:S(2)}) copy-start(s32[1,16]{1,0:T(1,128)} %refs_0_.1) | copy-start | bytes 196
  103.5 10.7 %copy-start.11 = (bf16[1024,384]{1,0:T(8,128)(2,1)S(1)}, bf16[1024,384]{1,0:T(8,128)(2,1)}, u32[]{:S(2)}) copy-start(bf16[1024,384]{1,0:T(8,128)(2,1)} %get-tuple-element.36) | copy-start | bytes 2359300
  105.7 74.0 %collective-permute-start.7 = (bf16[4,48,1792]{2,1,0:T(8,128)(2,1)}, bf16[4,48,1792]{2,1,0:T(8,128)(2,1)}, u32[]{:S(2)}, u32[]{:S(2)}) collective-permute-start(bf16[4,48,1792]{2,1,0:T(8,128)(2,1)} %get-tuple-element.89), channel_id=1, source_target_pairs={{0,2},{2,0},{4,6},{6,4},{8,10},{10,8},{12,14},{14,12},{16,18},{18,... | collective-permute-start | bytes 2064392 | tf_op jit(solution)/shard_map/ppermute | solution.py:108
  106.8 72.8 %collective-permute-start.8 = (bf16[4,48,1792]{2,1,0:T(8,128)(2,1)}, bf16[4,48,1792]{2,1,0:T(8,128)(2,1)}, u32[]{:S(2)}, u32[]{:S(2)}) collective-permute-start(bf16[4,48,1792]{2,1,0:T(8,128)(2,1)} %get-tuple-element.91), channel_id=1, source_target_pairs={{0,4},{2,6},{4,0},{6,2},{8,12},{10,14},{12,8},{14,10},{16,20},{18,... | collective-permute-start | bytes 2064392 | tf_op jit(solution)/shard_map/ppermute | solution.py:108
  107.7 71.9 %collective-permute-start.9 = (bf16[4,48,1792]{2,1,0:T(8,128)(2,1)}, bf16[4,48,1792]{2,1,0:T(8,128)(2,1)}, u32[]{:S(2)}, u32[]{:S(2)}) collective-permute-start(bf16[4,48,1792]{2,1,0:T(8,128)(2,1)} %get-tuple-element.90), channel_id=1, source_target_pairs={{0,6},{2,4},{4,2},{6,0},{8,14},{10,12},{12,10},{14,8},{16,22},{18,... | collective-permute-start | bytes 2064392 | tf_op jit(solution)/shard_map/ppermute | solution.py:108
  114.4 4.4 %copy-start = (bf16[1024,384]{1,0:T(8,128)(2,1)S(1)}, bf16[1024,384]{1,0:T(8,128)(2,1)}, u32[]{:S(2)}) copy-start(bf16[1024,384]{1,0:T(8,128)(2,1)} %get-tuple-element.37.k_ref) | copy-start | bytes 2359300
  114.5 4.4 %copy-start.1 = (f32[1024,128]{1,0:T(8,128)S(1)}, f32[1024,128]{1,0:T(8,128)}, u32[]{:S(2)}) copy-start(f32[1024,128]{1,0:T(8,128)} %get-tuple-element.39.cos_ref) | copy-start | bytes 1572868
  114.5 4.4 %copy-start.3 = (f32[3,2,1024]{2,1,0:T(2,128)S(1)}, f32[3,2,1024]{2,1,0:T(2,128)}, u32[]{:S(2)}) copy-start(f32[3,2,1024]{2,1,0:T(2,128)} %get-tuple-element.41.lse_ref) | copy-start | bytes 73732
  114.7 4.2 %copy-start.2 = (f32[1024,128]{1,0:T(8,128)S(1)}, f32[1024,128]{1,0:T(8,128)}, u32[]{:S(2)}) copy-start(f32[1024,128]{1,0:T(8,128)} %get-tuple-element.40.sin_ref) | copy-start | bytes 1572868
  164.8 23.1 %copy-start.7 = (f32[1024,768]{1,0:T(8,128)}, f32[1024,768]{1,0:T(8,128)S(1)}, u32[]{:S(2)}) copy-start(f32[1024,768]{1,0:T(8,128)S(1)} %fusion.1) | copy-start | bytes 9437188
  165.9 22.0 %collective-permute-start = (bf16[512,768]{1,0:T(8,128)(2,1)}, bf16[512,768]{1,0:T(8,128)(2,1)}, u32[]{:S(2)}, u32[]{:S(2)}) collective-permute-start(bf16[512,768]{1,0:T(8,128)(2,1)} %dynamic-slice_convert_fusion), channel_id=1, source_target_pairs={{0,1},{1,0},{2,3},{3,2},{4,5},{5,4},{6,7},{7,6},{8,9},{9,8},{10,11... | collective-permute-start | bytes 2359304 | tf_op jit(solution)/shard_map/ppermute | solution.py:122
  165.9 3.7 %copy-start.13 = (f32[512,128]{1,0:T(8,128)S(1)}, f32[512,128]{1,0:T(8,128)}, u32[]{:S(2)}) copy-start(f32[512,128]{1,0:T(8,128)} %get-tuple-element.33) | copy-start | bytes 786436
  165.9 3.9 %copy-start.19 = (bf16[1024,768]{1,0:T(8,128)(2,1)S(1)}, bf16[1024,768]{1,0:T(8,128)(2,1)}, u32[]{:S(2)}) copy-start(bf16[1024,768]{1,0:T(8,128)(2,1)} %get-tuple-element.47) | copy-start | bytes 4718596
  175.8 3.0 %copy-start.12 = (bf16[768,384]{1,0:T(8,128)(2,1)S(1)}, bf16[768,384]{1,0:T(8,128)(2,1)}, u32[]{:S(2)}) copy-start(bf16[768,384]{1,0:T(8,128)(2,1)} %convolution_convert_fusion.3) | copy-start | bytes 1769476
  179.6 8.3 %copy-start.5 = (f32[512,768]{1,0:T(8,128)S(1)}, f32[512,768]{1,0:T(8,128)}, u32[]{:S(2)}) copy-start(f32[512,768]{1,0:T(8,128)} %get-tuple-element.46) | copy-start | bytes 4718596
  181.8 0.8 copy-start.8
  183.5 15.8 %collective-permute-start.10 = (bf16[1,48,1792]{2,1,0:T(8,128)(2,1)}, bf16[1,48,1792]{2,1,0:T(8,128)(2,1)S(1)}, u32[]{:S(2)}, u32[]{:S(2)}) collective-permute-start(bf16[1,48,1792]{2,1,0:T(8,128)(2,1)} %get-tuple-element.95), channel_id=1, source_target_pairs={{0,8},{2,10},{4,12},{6,14},{8,0},{10,2},{12,4},{14,6},{16,24},{18,... | collective-permute-start | bytes 516104 | tf_op jit(solution)/shard_map/ppermute | solution.py:108
  184.7 16.1 %collective-permute-start.11 = (bf16[1,48,1792]{2,1,0:T(8,128)(2,1)}, bf16[1,48,1792]{2,1,0:T(8,128)(2,1)S(1)}, u32[]{:S(2)}, u32[]{:S(2)}) collective-permute-start(bf16[1,48,1792]{2,1,0:T(8,128)(2,1)} %get-tuple-element.97), channel_id=1, source_target_pairs={{0,16},{2,18},{4,20},{6,22},{8,24},{10,26},{12,28},{14,30},{16,0},... | collective-permute-start | bytes 516104 | tf_op jit(solution)/shard_map/ppermute | solution.py:108
  187.3 13.5 %collective-permute-start.12 = (bf16[1,48,1792]{2,1,0:T(8,128)(2,1)}, bf16[1,48,1792]{2,1,0:T(8,128)(2,1)}, u32[]{:S(2)}, u32[]{:S(2)}) collective-permute-start(bf16[1,48,1792]{2,1,0:T(8,128)(2,1)} %get-tuple-element.96), channel_id=1, source_target_pairs={{0,24},{2,26},{4,28},{6,30},{8,16},{10,18},{12,20},{14,22},{16,8},... | collective-permute-start | bytes 516104 | tf_op jit(solution)/shard_map/ppermute | solution.py:108
  193.7 2.3 copy-start.6
  193.7 2.3 copy-start.9
  193.9 17.4 %collective-permute-start.1 = (bf16[4,48,1664]{2,1,0:T(8,128)(2,1)S(1)}, bf16[4,48,1664]{2,1,0:T(8,128)(2,1)S(1)}, u32[]{:S(2)}, u32[]{:S(2)}) collective-permute-start(bf16[4,48,1664]{2,1,0:T(8,128)(2,1)S(1)} %get-tuple-element.92), channel_id=1, source_target_pairs={{0,2},{2,0},{4,6},{6,4},{8,10},{10,8},{12,14},{14,12},{16,18},{18,... | collective-permute-start | bytes 1916936 | tf_op jit(solution)/shard_map/ppermute | solution.py:108
  195.1 29.2 %collective-permute-start.2 = (bf16[4,48,1664]{2,1,0:T(8,128)(2,1)S(1)}, bf16[4,48,1664]{2,1,0:T(8,128)(2,1)S(1)}, u32[]{:S(2)}, u32[]{:S(2)}) collective-permute-start(bf16[4,48,1664]{2,1,0:T(8,128)(2,1)S(1)} %get-tuple-element.94), channel_id=1, source_target_pairs={{0,4},{2,6},{4,0},{6,2},{8,12},{10,14},{12,8},{14,10},{16,20},{18,... | collective-permute-start | bytes 1916936 | tf_op jit(solution)/shard_map/ppermute | solution.py:108
  199.3 25.0 %collective-permute-start.3 = (bf16[4,48,1664]{2,1,0:T(8,128)(2,1)S(1)}, bf16[4,48,1664]{2,1,0:T(8,128)(2,1)S(1)}, u32[]{:S(2)}, u32[]{:S(2)}) collective-permute-start(bf16[4,48,1664]{2,1,0:T(8,128)(2,1)S(1)} %get-tuple-element.93), channel_id=1, source_target_pairs={{0,6},{2,4},{4,2},{6,0},{8,14},{10,12},{12,10},{14,8},{16,22},{18,... | collective-permute-start | bytes 1916936 | tf_op jit(solution)/shard_map/ppermute | solution.py:108
  224.7 6.4 %collective-permute-start.4 = (bf16[1,48,1664]{2,1,0:T(8,128)(2,1)S(1)}, bf16[1,48,1664]{2,1,0:T(8,128)(2,1)S(1)}, u32[]{:S(2)}, u32[]{:S(2)}) collective-permute-start(bf16[1,48,1664]{2,1,0:T(8,128)(2,1)S(1)} %get-tuple-element.98), channel_id=1, source_target_pairs={{0,8},{2,10},{4,12},{6,14},{8,0},{10,2},{12,4},{14,6},{16,24},{18,... | collective-permute-start | bytes 479240 | tf_op jit(solution)/shard_map/ppermute | solution.py:108
  225.1 14.4 %collective-permute-start.5 = (bf16[1,48,1664]{2,1,0:T(8,128)(2,1)S(1)}, bf16[1,48,1664]{2,1,0:T(8,128)(2,1)S(1)}, u32[]{:S(2)}, u32[]{:S(2)}) collective-permute-start(bf16[1,48,1664]{2,1,0:T(8,128)(2,1)S(1)} %get-tuple-element.100), channel_id=1, source_target_pairs={{0,16},{2,18},{4,20},{6,22},{8,24},{10,26},{12,28},{14,30},{16,0},... | collective-permute-start | bytes 479240 | tf_op jit(solution)/shard_map/ppermute | solution.py:108
  228.6 10.9 %collective-permute-start.6 = (bf16[1,48,1664]{2,1,0:T(8,128)(2,1)S(1)}, bf16[1,48,1664]{2,1,0:T(8,128)(2,1)S(1)}, u32[]{:S(2)}, u32[]{:S(2)}) collective-permute-start(bf16[1,48,1664]{2,1,0:T(8,128)(2,1)S(1)} %get-tuple-element.99), channel_id=1, source_target_pairs={{0,24},{2,26},{4,28},{6,30},{8,16},{10,18},{12,20},{14,22},{16,8},... | collective-permute-start | bytes 479240 | tf_op jit(solution)/shard_map/ppermute | solution.py:108
  229.2 12.8 %copy-start.10 = (f32[512,768]{1,0:T(8,128)S(1)}, f32[512,768]{1,0:T(8,128)}, u32[]{:S(2)}) copy-start(f32[512,768]{1,0:T(8,128)} %get-tuple-element.125) | copy-start | bytes 4718596
  239.7 1.7 collective-permute-start.13
where the time goes:
time: 244 us; the launch traced here: 243 us
  Pallas kernels  116 us (48%)
  local copies, waits for them, and re-layouts  42 us (17%)
  waiting for transfers between devices  30.9 us (13%)
  matrix products  19.9 us (8%)
  starting transfers between devices  16 us (7%)
  other arithmetic  14.8 us (6%)
  between operations  3.84 us (2%)
    pallas_call x1, Pallas kernels, call_front(): pl.pallas_call(functools.partial(front_kernel, names, spans), out_shape=[...  82 us
    pallas_call x1, Pallas kernels, attention_backward(): pl.pallas_call(backward_kernel, grid=(pairs,), out_shape=(low, low, low),...  33.7 us
    ppermute x12, waiting for transfers between devices, sum_blocks(): lax.ppermute(pick(mine ^ step), 'dp', swap_pairs(count, step * stride))  30.9 us
    ppermute x12, starting transfers between devices, sum_blocks(): lax.ppermute(pick(mine ^ step), 'dp', swap_pairs(count, step * stride))  15.9 us
    dot_general x4, matrix products, dot_tn(): lax.dot_general(left, right, (((0,), (0,)), ((), ())), preferred_element_...  14.5 us
    concatenate x6, local copies, waits for them, and re-layouts, padded(): return jnp.concatenate(pieces, axis=1)  13.4 us
    unnamed x50, local copies, waits for them, and re-layouts  10.7 us
    dot_general x1, matrix products, dot_nt(): lax.dot_general(left, right, (((1,), (1,)), ((), ())), preferred_element_...  5.44 us
  transfers between devices with their start and end apart: 14, of which 4 were waited for; matrix products, arithmetic and copies ran while one was open for 21% of the time, Pallas kernels for 14%

commit v1 on v0

--- a/solution.py
+++ b/solution.py
@@ -543,6 +543,7 @@
     def finish(self):
         for copy in self.started:
             copy.wait_send()
+        self.started = []
 
 
 class Gather(Links):
@@ -603,6 +604,81 @@
         )
 
 
+class Scatter:
+    def __init__(self, link, chunks):
+        self.link = link
+        self.ref = link.ref
+        self.chunks = chunks
+        self.got = {}
+
+    def send(self, name, stage, moves):
+        sems = (self.ref.sum_out, self.ref.sum_in)
+        place = 7 * list(self.chunks).index(name) + 2 * stage
+        copies = [
+            self.link.copy(source, target, sems, place + step, (side, self.link.core))
+            for step, (source, target, side) in enumerate(moves)
+        ]
+        self.link.start(*copies)
+        self.got[name] = copies
+
+    def arrive(self, name):
+        for copy in self.got[name]:
+            copy.wait_recv()
+
+    def parts(self, name):
+        held, span, place = self.chunks[name]
+        return held, pl.ds(*span), pl.ds(place, span[1])
+
+    def one(self, name):
+        link, ref = self.link, self.ref
+        held, cols, to = self.parts(name)
+        both = pl.ds(0, 2)
+        self.send(name, 0, [
+            (held.at[pl.ds(0, 2), 1 - link.y, both, :, cols], ref.low_one.at[:, :, :, to], link.y_side),
+            (held.at[pl.ds(2, 2), both, 1 - link.x, :, cols], ref.high_one.at[:, :, :, to], link.x_side),
+        ])
+
+    def two(self, name):
+        link, ref = self.link, self.ref
+        held, cols, to = self.parts(name)
+        both = pl.ds(0, 2)
+        self.arrive(name)
+        at = (pl.ds(0, 2), link.y, both, slice(None), cols)
+        held[at] = held[at] + ref.low_one[:, :, :, to]
+        at = (pl.ds(2, 2), both, link.x, slice(None), cols)
+        held[at] = held[at] + ref.high_one[:, :, :, to]
+        self.send(name, 1, [
+            (held.at[pl.ds(0, 2), link.y, 1 - link.x, :, cols], ref.low_two.at[:, :, to], link.x_side),
+            (held.at[pl.ds(2, 2), 1 - link.y, link.x, :, cols], ref.high_two.at[:, :, to], link.y_side),
+        ])
+
+    def three(self, name):
+        link, ref = self.link, self.ref
+        held, cols, to = self.parts(name)
+        self.arrive(name)
+        at = (pl.ds(0, 2), link.y, link.x, slice(None), cols)
+        held[at] = held[at] + ref.low_two[:, :, to]
+        at = (pl.ds(2, 2), link.y, link.x, slice(None), cols)
+        held[at] = held[at] + ref.high_two[:, :, to]
+        self.send(name, 2, [
+            (
+                held.at[link.z_of[step], link.y, link.x, :, cols],
+                ref.far_sum.at[step - 1, :, to],
+                link.z_side[step],
+            )
+            for step in (1, 2, 3)
+        ])
+
+    def four(self, name):
+        link, ref = self.link, self.ref
+        held, cols, to = self.parts(name)
+        self.arrive(name)
+        total = held[link.z, link.y, link.x, :, cols].astype(jnp.float32)
+        for step in range(3):
+            total = total + ref.far_sum[step, :, to].astype(jnp.float32)
+        ref.sums[:, to] = total
+
+
 def weights_at(full, span):
     block = full[:, :, :, :, span[0] : span[0] + span[1]]
     return block.reshape(-1, span[1])
@@ -617,7 +693,7 @@
     return wrap
 
 
-def front_kernel(names, spans, *refs):
+def layer_kernel(names, spans, *refs):
     ref = types.SimpleNamespace(**dict(zip(names, refs)))
     half, width = ref.tok.shape
     rows = 2 * half
@@ -633,6 +709,26 @@
     own_at = core * half
     other_at = (1 - core) * half
     part = 256
+
+    ref.grad_low = ref.normed
+    ref.grad_rolled = ref.context_rolled
+    scatter = Scatter(
+        link,
+        {
+            "inner": (ref.full, (spans["gate"][0], 2 * main + LANES), spans["gate"][0]),
+            "mlp": (ref.full, spans["mlp"], spans["mlp"][0]),
+            "out": (ref.full, spans["out"], spans["out"][0]),
+            **{
+                "pair%d" % pair: (
+                    ref.grad_qkv,
+                    (3 * LANES * pair, 3 * LANES),
+                    spans["pair%d" % pair][0],
+                )
+                for pair in range(pairs)
+            },
+            "gains": (ref.full, spans["gains"], spans["gains"][0]),
+        },
+    )
 
     link.enter()
     ref.full[link.z, link.y, link.x] = ref.pack[...]
@@ -785,13 +881,13 @@
     link.send_two("gate")
     link.arrive("out")
 
-    def pair_sum(product, place, keep):
+    def pair_sum(product, place, sem, keep):
         @row_loop(half, part)
         def _(at):
             there = pl.ds(pl.multiple_of(other_at + at.start, part), part)
             ref.sent[place, at, :] = product(there).astype(jnp.bfloat16)
 
-        got = link.to_core(ref.sent.at[place], ref.taken.at[place], 2 + place)
+        got = link.to_core(ref.sent.at[place], ref.taken.at[place], sem)
 
         @row_loop(half, part)
         def _(at):
@@ -801,7 +897,7 @@
         return got
 
     got_attended = pair_sum(
-        lambda at: dot_nt(ref.context[at, :], weights_at(ref.full, spans["out"])), 0, ref.hidden
+        lambda at: dot_nt(ref.context[at, :], weights_at(ref.full, spans["out"])), 0, 2, ref.hidden
     )
     got_attended.wait_recv()
 
@@ -856,11 +952,23 @@
 
     inner = (spans["gate"][0], 2 * main + LANES)
     got_normed_two = pair_sum(
-        lambda at: dot_nt(ref.grad_gate_up[at, :], weights_at(ref.full, inner)), 1, ref.grad_hidden
-    )
-    got_branch = pair_sum(
-        lambda at: dot_nt(ref.product[at, :], weights_at(ref.full, spans["mlp"])), 2, ref.outputs
-    )
+        lambda at: dot_nt(ref.grad_gate_up[at, :], weights_at(ref.full, inner)), 1, 3, ref.grad_hidden
+    )
+    link.finish()
+
+    def weight_grad(left, right, held, first):
+        wide = right.shape[1]
+
+        @pl.loop(0, 2)
+        def _(step):
+            cols = pl.ds(pl.multiple_of(step * (width // 2), LANES), width // 2)
+            block = dot_tn(left[:, cols], right[...]).astype(jnp.bfloat16)
+            held[pl.ds(2 * step, 2), :, :, :, first : first + wide] = block.reshape(
+                2, 2, 2, width // 16, wide
+            )
+
+    weight_grad(ref.normed_mlp, ref.grad_gate_up, ref.full, inner[0])
+    scatter.one("inner")
     got_normed_two.wait_recv()
     ref.gain_rows[...] = jnp.zeros_like(ref.gain_rows)
 
@@ -877,6 +985,28 @@
         ref.grad_low[here, :] = grad.astype(jnp.bfloat16)
 
     got_low = link.to_core(ref.grad_low.at[own, :], ref.grad_low.at[own, :], 7)
+    got_branch = pair_sum(
+        lambda at: dot_nt(ref.product[at, :], weights_at(ref.full, spans["mlp"])), 2, 4, ref.outputs
+    )
+    weight_grad(ref.grad_rows, ref.product, ref.full, spans["mlp"][0])
+    scatter.one("mlp")
+    scatter.two("inner")
+    got_low.wait_recv()
+
+    @row_loop(rows, part)
+    def _(at):
+        ref.grad_context[at, :] = dot_nn(
+            ref.grad_low[at, :], weights_at(ref.full, spans["out"])
+        ).astype(jnp.bfloat16)
+
+    @row_loop(rows, part)
+    def _(at):
+        ref.grad_rolled[at, :] = dot_nn(ref.perm[at, :], ref.grad_context[...]).astype(jnp.bfloat16)
+
+    weight_grad(ref.grad_low, ref.context, ref.full, spans["out"][0])
+    scatter.one("out")
+    scatter.two("mlp")
+    scatter.three("inner")
     got_branch.wait_recv()
 
     @row_loop(half, 128)
@@ -885,12 +1015,140 @@
             ref.outputs[at, :] + ref.hidden[at, :] + ref.taken[2, at, :].astype(jnp.float32)
         )
 
-    got_low.wait_recv()
-    ref.weights[...] = weights_at(ref.full, spans["total"])
+    def pull(pair, first):
+        cols = slice(pair * LANES, (pair + 1) * LANES)
+        base = 0 if first else half
+        span = slice(base, base + half)
+
+        @row_loop(half, part)
+        def _(at):
+            at = pl.ds(pl.multiple_of(base + at.start, part), part)
+            ref.keys_t[:, at] = ref.keys[at, cols].astype(jnp.float32).T.astype(jnp.bfloat16)
+
+        @pl.loop(0, half // part)
+        def _(step):
+            at = pl.ds(pl.multiple_of(base + step * part, part), part)
+            lane = lax.broadcasted_iota(jnp.int32, (part, LANES), 1)
+            query_pair = ref.queries[at, cols]
+            grad_pair = ref.grad_rolled[at, cols]
+            parts, all_probs, all_grads, all_queries, all_pulls = [], [], [], [], []
+            for head in range(LANES // HEAD_DIM):
+                query = jnp.where(lane // HEAD_DIM == head, query_pair, 0)
+                grad = jnp.where(lane // HEAD_DIM == head, grad_pair, 0)
+                scores = dot_nt(ref.keys[span, cols], query)
+                if not first:
+                    scores = scores + ref.bias[:, pl.ds(pl.multiple_of(step * part, part), part)]
+                probs = jnp.exp(scores - ref.lse[pair, head : head + 1, at])
+                grad_probs = dot_nt(ref.values[span, cols], grad)
+                weighted = probs * grad_probs
+                drop = jnp.sum(weighted, axis=0, keepdims=True)
+                pulled = (weighted - probs * drop).astype(jnp.bfloat16)
+                all_probs.append(probs.astype(jnp.bfloat16))
+                all_grads.append(grad)
+                all_queries.append(query)
+                all_pulls.append(pulled)
+                parts.append(
+                    dot_nn(ref.keys_t[head * HEAD_DIM : (head + 1) * HEAD_DIM, span], pulled)
+                )
+            grad_values = dot_nn(
+                jnp.concatenate(all_probs, axis=1), jnp.concatenate(all_grads, axis=0)
+            )
+            grad_keys = dot_nn(
+                jnp.concatenate(all_pulls, axis=1), jnp.concatenate(all_queries, axis=0)
+            )
+
+            @pl.when(step == 0)
+            def _():
+                ref.acc[span, LANES : 2 * LANES] = grad_keys
+                ref.acc[span, 2 * LANES :] = grad_values
+
+            @pl.when(step > 0)
+            def _():
+                ref.acc[span, LANES : 2 * LANES] += grad_keys
+                ref.acc[span, 2 * LANES :] += grad_values
+
+            ref.acc[at, :LANES] = jnp.concatenate(parts, axis=0).T
+
+    def unproject(pair):
+        first = 3 * LANES * pair
+
+        @row_loop(rows, part)
+        def _(at):
+            lane = lax.broadcasted_iota(jnp.int32, (part, LANES), 1)
+            cosine, sine = ref.cosine[at, :], -ref.sine[at, :]
+            grad_query = turn(ref.acc[at, :LANES], cosine, sine, lane) * SCALE
+            grad_key = turn(ref.acc[at, LANES : 2 * LANES], cosine, sine, lane)
+            ref.grad_three[at, :LANES] = grad_query.astype(jnp.bfloat16)
+            ref.grad_three[at, LANES : 2 * LANES] = grad_key.astype(jnp.bfloat16)
+            ref.grad_three[at, 2 * LANES :] = ref.acc[at, 2 * LANES :].astype(jnp.bfloat16)
+
+        weight_grad(ref.rolled, ref.grad_three, ref.grad_qkv, first)
+        scatter.one("pair%d" % pair)
+
+        @row_loop(rows, part)
+        def _(at):
+            ref.grad_projected[at, first : first + 3 * LANES] = dot_nn(
+                ref.perm_back[at, :], ref.grad_three[...]
+            ).astype(jnp.bfloat16)
+
+    pull(0, True)
+    scatter.two("out")
+    scatter.three("mlp")
+    pull(0, False)
+    scatter.four("inner")
+    unproject(0)
+    scatter.three("out")
+    pull(1, True)
+    scatter.two("pair0")
+    scatter.four("mlp")
+    pull(1, False)
+    scatter.three("pair0")
+    unproject(1)
+    scatter.four("out")
+    pull(2, True)
+    scatter.two("pair1")
+    scatter.four("pair0")
+    pull(2, False)
+    scatter.three("pair1")
+    unproject(2)
+    qkv_span = (spans["pair0"][0], 3 * pairs * LANES)
+    got_one = pair_sum(
+        lambda at: dot_nt(ref.grad_projected[at, :], weights_at(ref.full, qkv_span)),
+        0, 5, ref.grad_tokens,
+    )
+    scatter.two("pair2")
+    scatter.four("pair1")
+    got_one.wait_recv()
+
+    @row_loop(half, 128)
+    def _(at):
+        incoming = ref.grad_tokens[at, :] + ref.taken[0, at, :].astype(jnp.float32)
+        unit = ref.unit_one[at, :]
+        ref.gain_rows[0:1, :] += jnp.sum(incoming * unit, axis=0, keepdims=True)
+        ref.grad_tokens[at, :] = ref.grad_hidden[at, :] + norm_backward(
+            incoming, ref.gain[0:1, :], unit, ref.scale_one[at, 0:1]
+        )
+
+    got_gain = link.to_core(ref.gain_rows, ref.gain_other, 8)
+    scatter.three("pair2")
+    got_gain.wait_recv()
+    gain_rows = ref.gain_rows[...] + ref.gain_other[...]
+    high = gain_rows.astype(jnp.bfloat16)
+    rest = (gain_rows - high.astype(jnp.float32)).astype(jnp.bfloat16)
+    slot = lax.broadcasted_iota(jnp.int32, (16, LANES), 0)
+    lane = lax.broadcasted_iota(jnp.int32, (16, LANES), 1)
+    pick = jnp.where(slot == lane, 1.0, 0.0).astype(jnp.bfloat16)
+    columns = dot_tn(jnp.concatenate([high, rest], axis=0), pick).astype(jnp.bfloat16)
+    ref.full[:, :, :, :, 0:LANES] = columns.reshape(4, 2, 2, width // 16, LANES)
+    scatter.one("gains")
+    scatter.four("pair2")
+    scatter.two("gains")
+    scatter.three("gains")
+    scatter.four("gains")
     link.finish()
 
 
-def call_front(pack, tokens, cotangent, offsets, spans):
+def call_layer(pack, tokens, cotangent, offsets, spans):
     half, width = tokens.shape
     rows = 2 * half
     height, total = pack.shape
@@ -905,58 +1163,70 @@
     low, wide = jnp.bfloat16, jnp.float32
     outs = dict(
         outputs=((half, width), wide),
-        grad_hidden=((half, width), wide),
-        gain_rows=((8, width), wide),
-        gain=((8, width), wide),
-        unit_one=((half, width), wide),
-        scale_one=((half, LANES), wide),
-        cosine=((rows, LANES), wide),
-        sine=((rows, LANES), wide),
-        lse=((pairs, LANES // HEAD_DIM, rows), wide),
+        grad_tokens=((half, width), wide),
+        sums=((height, total), wide),
+    )
+    chunk_count = 1 + pairs + 4
+    kept = dict(
+        full=((4, 2, 2, height, total), low),
+        grad_qkv=((4, 2, 2, height, 3 * width_here), low),
+        low_one=((2, 2, height, total), low),
+        high_one=((2, 2, height, total), low),
+        low_two=((2, height, total), low),
+        high_two=((2, height, total), low),
+        far_sum=((3, height, total), low),
+        normed=((rows, width), low),
         rolled=((rows, width), low),
+        grad_rows=((rows, width), low),
+        normed_mlp=((rows, width), low),
+        perm=((rows, rows), low),
+        perm_back=((rows, rows), low),
+        bias=((half, half), wide),
+        values_t=((LANES, rows), low),
+        keys_t=((LANES, rows), low),
         queries=((rows, width_here), low),
         keys=((rows, width_here), low),
         values=((rows, width_here), low),
         context=((rows, width_here), low),
-        grad_rows=((rows, width), low),
-        normed_mlp=((rows, width), low),
+        context_rolled=((rows, width_here), low),
+        grad_context=((rows, width_here), low),
+        grad_three=((rows, 3 * LANES), low),
+        grad_projected=((rows, 3 * width_here), low),
+        acc=((rows, 3 * LANES), wide),
+        lse=((pairs, LANES // HEAD_DIM, rows), wide),
         product=((rows, main + LANES), low),
         grad_gate_up=((rows, 2 * main + LANES), low),
-        grad_low=((rows, width), low),
-        weights=((width, total), low),
-    )
-    chunk_count = 1 + pairs + 4
-    scratch = dict(
-        full=pltpu.VMEM((4, 2, 2, height, total), low),
-        normed=pltpu.VMEM((rows, width), low),
-        perm=pltpu.VMEM((rows, rows), low),
-        perm_back=pltpu.VMEM((rows, rows), low),
-        bias=pltpu.VMEM((half, half), wide),
-        values_t=pltpu.VMEM((LANES, rows), low),
-        context_rolled=pltpu.VMEM((rows, width_here), low),
-        sent=pltpu.VMEM((3, half, width), low),
-        taken=pltpu.VMEM((3, half, width), low),
-        hidden=pltpu.VMEM((half, width), wide),
-        unit_two=pltpu.VMEM((half, width), wide),
-        scale_two=pltpu.VMEM((half, LANES), wide),
-        grad_product=pltpu.VMEM((rows, main + LANES), wide),
-        far_out=pltpu.SemaphoreType.DMA((3 * chunk_count,)),
-        far_in=pltpu.SemaphoreType.DMA((3 * chunk_count,)),
-        near_out=pltpu.SemaphoreType.DMA((4 * chunk_count,)),
-        near_in=pltpu.SemaphoreType.DMA((4 * chunk_count,)),
-        core_out=pltpu.SemaphoreType.DMA((8,)),
-        core_in=pltpu.SemaphoreType.DMA((8,)),
-    )
+        grad_product=((rows, main + LANES), wide),
+        sent=((3, half, width), low),
+        taken=((3, half, width), low),
+        hidden=((half, width), wide),
+        grad_hidden=((half, width), wide),
+        unit_one=((half, width), wide),
+        unit_two=((half, width), wide),
+        scale_one=((half, LANES), wide),
+        scale_two=((half, LANES), wide),
+        cosine=((rows, LANES), wide),
+        sine=((rows, LANES), wide),
+        gain=((8, width), wide),
+        gain_rows=((8, width), wide),
+        gain_other=((8, width), wide),
+    )
+    scratch = {name: pltpu.VMEM(*entry) for name, entry in kept.items()}
+    for name, count in (
+        ("far", 3 * chunk_count), ("near", 4 * chunk_count), ("core", 9), ("sum", 7 * (pairs + 4)),
+    ):
+        scratch[name + "_out"] = pltpu.SemaphoreType.DMA((count,))
+        scratch[name + "_in"] = pltpu.SemaphoreType.DMA((count,))
     names = ["offsets", "pack", "tok", "cot", "inverse"] + list(outs) + list(scratch)
     vmem = pl.BlockSpec(memory_space=pltpu.VMEM)
     results = pl.pallas_call(
-        functools.partial(front_kernel, names, spans),
+        functools.partial(layer_kernel, names, spans),
         out_shape=[jax.ShapeDtypeStruct(*entry) for entry in outs.values()],
         in_specs=[pl.BlockSpec(memory_space=pltpu.SMEM)] + [vmem] * 4,
         out_specs=[vmem] * len(outs),
         scratch_shapes=list(scratch.values()),
         compiler_params=pltpu.CompilerParams(
-            collective_id=0, has_side_effects=True, vmem_limit_bytes=60 * 1024 * 1024
+            collective_id=0, has_side_effects=True, vmem_limit_bytes=63 * 1024 * 1024
         ),
         cost_estimate=pl.CostEstimate(
             flops=12 * 10**9, bytes_accessed=30 * 10**6, transcendentals=10**7
@@ -974,68 +1244,24 @@
     main = hidden_here // LANES * LANES
     spans = fast_columns(width_here, hidden_here)
     pack = pack_shards(w_qkv, w_attn_out, w_in, w_mlp_out, gain_attn, gain_mlp)
-    f = call_front(pack, tokens, cotangent, offsets, spans)
-    core = lax.axis_index("tensor")
-    shift = seq_starts(offsets[0], jnp.full((1,), half - 1, jnp.int32))[0]
-    place = (jnp.arange(rows, dtype=jnp.int32) + shift) % rows
-    starts = seq_starts(offsets[0], place)
-    pick = lambda name: f.weights[:, spans[name][0] : spans[name][0] + spans[name][1]]
-    grads_three = attention_backward(
-        jnp.roll(f.grad_low, -shift, axis=0), pick("out"), f.queries * 8, f.keys, f.values,
-        f.cosine, f.sine, starts, f.lse,
-    )
-    grad_projected = jnp.concatenate(
-        [g[:, p * LANES : (p + 1) * LANES] for p in range(pairs) for g in grads_three], axis=1
-    )
+    f = call_layer(pack, tokens, cotangent, offsets, spans)
+    pick = lambda name: f.sums[:, spans[name][0] : spans[name][0] + spans[name][1]]
     at = spans["pair0"][0]
-    qkv_full = f.weights[:, at : at + 3 * width_here]
-    mlp_terms = padded(
-        [
-            dot_tn(f.normed_mlp, f.grad_gate_up).astype(jnp.bfloat16),
-            dot_tn(f.grad_rows, f.product[:, :hidden_here]).astype(jnp.bfloat16),
-            two_terms(f.gain_rows[1]),
-        ]
-    )
-    mlp_sums = sum_blocks(mlp_terms)
-    partial_one = dot_nt(jnp.roll(grad_projected, shift, axis=0), qkv_full)
-    mine = lax.dynamic_slice_in_dim(partial_one, core * half, half, 0)
-    other = lax.dynamic_slice_in_dim(partial_one, (1 - core) * half, half, 0)
-    grad_normed_one = mine + other_half(other.astype(jnp.bfloat16)).astype(jnp.float32)
-    grad_tokens = f.grad_hidden + norm_backward(
-        grad_normed_one, f.gain[0:1], f.unit_one, f.scale_one[:, 0:1]
-    )
-    attn_terms = padded(
-        [
-            dot_tn(f.rolled, grad_projected).astype(jnp.bfloat16),
-            dot_tn(f.grad_low, f.context).astype(jnp.bfloat16),
-            two_terms(jnp.sum(grad_normed_one * f.unit_one, axis=0)),
-        ]
-    )
-    attn_sums = sum_blocks(attn_terms)
-    gain_one_cols = attn_sums[:, 4 * width_here : 4 * width_here + 2].sum(axis=1)
-    gain_two_cols = mlp_sums[:, 3 * hidden_here : 3 * hidden_here + 2].sum(axis=1)
-    gains = jnp.stack([gain_one_cols, gain_two_cols])
-    gains = gains + other_half(gains)
-    tail = mlp_sums[:, 2 * main : 2 * hidden_here]
-    grad_in = jnp.stack(
-        [
-            jnp.concatenate([mlp_sums[:, :main], tail[:, : hidden_here - main]], axis=1),
-            jnp.concatenate([mlp_sums[:, main : 2 * main], tail[:, hidden_here - main :]], axis=1),
-        ],
-        axis=1,
-    )
+    tail = pick("tail")
+    gate = jnp.concatenate([pick("gate"), tail[:, : hidden_here - main]], axis=1)
+    up = jnp.concatenate([pick("up"), tail[:, hidden_here - main :]], axis=1)
     return (
         f.outputs,
-        grad_tokens,
-        attn_sums[:, : 3 * width_here]
+        f.grad_tokens,
+        f.sums[:, at : at + 3 * width_here]
         .reshape(height, pairs, 3, LANES)
         .transpose(0, 2, 1, 3)
         .reshape(height, 3, width_here),
-        attn_sums[:, 3 * width_here : 4 * width_here].T,
-        grad_in,
-        mlp_sums[:, 2 * hidden_here : 3 * hidden_here].T,
-        gains[0],
-        gains[1],
+        pick("out").T,
+        jnp.stack([gate, up], axis=1),
+        pick("mlp")[:, :hidden_here].T,
+        f.sums[:, 0] + f.sums[:, 8],
+        f.sums[:, 1] + f.sums[:, 9],
     )
 
 

time: 244 us -> 168 us (0.69)
  Pallas kernels: 116 us -> 153 us
  waiting for transfers between devices: 30.9 us -> 0 us
  local copies, waits for them, and re-layouts: 42 us -> 13.5 us
  matrix products: 19.9 us -> 0 us
  starting transfers between devices: 16 us -> 0 us
  other arithmetic: 14.8 us -> 0.76 us
  between operations: 3.84 us -> 0.79 us
    pallas_call x2 -> x1, Pallas kernels: 116 us -> 153 us  [call_layer(): pl.pallas_call(functools.partial(layer_kernel, names, spans), out_shape=[...]
    ppermute x14 -> x0, waiting for transfers between devices: 30.9 us -> none  [the longest x12 30.9 us: sum_blocks(): lax.ppermute(pick(mine ^ step), 'dp', swap_pairs(count, step * stride))]
    dot_general x5 -> x0, matrix products: 19.9 us -> none  [the longest x4 14.5 us: dot_tn(): lax.dot_general(left, right, (((0,), (0,)), ((), ())), preferred_element_...]
    ppermute x14 -> x0, starting transfers between devices: 16 us -> none  [the longest x12 15.9 us: sum_blocks(): lax.ppermute(pick(mine ^ step), 'dp', swap_pairs(count, step * stride))]
    concatenate x7 -> x0, local copies, waits for them, and re-layouts: 14.1 us -> none  [the longest x6 13.4 us: padded(): return jnp.concatenate(pieces, axis=1)]
    unnamed x50 -> x13, local copies, waits for them, and re-layouts: 10.7 us -> 3.95 us
    concatenate x1 -> x0, other arithmetic: 4.16 us -> none  [fast_shards(): jnp.roll(f.grad_low, -shift, axis=0)]
    squeeze x6 -> x0, local copies, waits for them, and re-layouts: 2.97 us -> none  [the longest x4 2.37 us: sum_blocks(): lax.dynamic_index_in_dim(parts, place, 1, keepdims=False)]
  transfers between devices with their start and end apart: 14 -> 0, of which waited for: 4 -> 0; matrix products, arithmetic and copies ran while one was open for 21% -> 0% of each run, Pallas kernels for 14% -> 0%
where the time goes in v1:
time: 168 us
  Pallas kernels  153 us (91%)
  local copies, waits for them, and re-layouts  13.5 us (8%)
    pallas_call x1, Pallas kernels, call_layer(): pl.pallas_call(functools.partial(layer_kernel, names, spans), out_shape=[...  153 us
    unnamed x13, local copies, waits for them, and re-layouts  3.95 us

profile of v1, /device:TPU:0, one launch (start us, length us, event | category | flops | bytes accessed | tf_op | source)
XLA Modules:
  0.0 168.1 jit_solution(7652335886369090207)
XLA Ops:
  0.6 0.0 copy-start.4
  0.6 0.0 copy-start.3
  0.7 0.8 copy.31
  1.4 0.8 copy.32
  2.2 0.9 reshape.35
  3.1 0.1 copy.26
  3.3 0.1 reshape.36
  3.4 1.1 fusion.3
  4.5 0.9 fusion.2
  5.4 0.0 copy-done.4
  5.4 0.0 copy-done.3
  5.4 0.8 concatenate.9.refs_1_
  6.3 0.6 broadcast_in_dim_tile.3.refs_4_
  6.9 153.0 %shard_map.152 = (f32[512,768]{1,0:T(8,128)}, f32[512,768]{1,0:T(8,128)}, f32[48,3456]{1,0:T(8,128)}) custom-call(s32[1,16]{1,0:T(1,128)} %refs_0_.1, bf16[48,3456]{1,0:T(8,128)(2,1)} %concatenate.9.refs_1_, f32[512,768]{1,0:T(8,128)} %refs_2_.1, f32[512,768]{1,0:T(8,128)} %refs_3_.1, f32[1,128]{1,0:T(1,128)} %broadcast_in_dim_tile.3.refs_4_), custom_call_target="tpu_custom_call" | custom-call | flops 12000000000 | bytes 30000000 | tf_op jit(solution)/shard_map/pallas_call | solution.py:1222
  159.9 0.0 copy-start.2
  160.0 1.0 slice.54
  161.0 0.1 reshape.37
  161.1 0.1 copy.33
  161.2 0.0 copy-start.1
  161.2 0.8 reshape.38
  162.0 0.0 copy-done.2
  162.0 0.6 slice_bitcast_fusion.1
  162.6 0.1 fusion.1
  162.8 0.8 copy.34
  163.6 0.7 slice_bitcast_fusion
  164.3 0.7 add_reduce_fusion
  165.0 0.0 copy-done.1
  165.0 0.0 copy-start
  165.0 1.1 copy.45
  166.1 0.8 copy-done
  166.9 1.1 copy.46
  (10 shorter events, 0.1 us)
Async XLA Ops:
  0.6 4.8 %copy-start.4 = (bf16[384,48]{0,1:T(8,128)(2,1)S(1)}, bf16[384,48]{0,1:T(8,128)(2,1)}, u32[]{:S(2)}) copy-start(bf16[384,48]{0,1:T(8,128)(2,1)} %param.12) | copy-start | bytes 110596
  0.6 4.8 %copy-start.3 = (bf16[576,48]{0,1:T(8,128)(2,1)S(1)}, bf16[576,48]{0,1:T(8,128)(2,1)}, u32[]{:S(2)}) copy-start(bf16[576,48]{0,1:T(8,128)(2,1)} %param.14) | copy-start | bytes 165892
  159.9 2.0 %copy-start.2 = (f32[48,3456]{1,0:T(8,128)S(1)}, f32[48,3456]{1,0:T(8,128)}, u32[]{:S(2)}) copy-start(f32[48,3456]{1,0:T(8,128)} %get-tuple-element.13) | copy-start | bytes 1990660
  161.2 3.8 %copy-start.1 = (f32[512,768]{1,0:T(8,128)S(1)}, f32[512,768]{1,0:T(8,128)}, u32[]{:S(2)}) copy-start(f32[512,768]{1,0:T(8,128)} %get-tuple-element.52) | copy-start | bytes 4718596
  165.0 2.0 %copy-start = (f32[512,768]{1,0:T(8,128)S(1)}, f32[512,768]{1,0:T(8,128)}, u32[]{:S(2)}) copy-start(f32[512,768]{1,0:T(8,128)} %get-tuple-element.53) | copy-start | bytes 4718596

commit v2 on v1

--- a/solution.py
+++ b/solution.py
@@ -711,17 +711,20 @@
     part = 256
 
     ref.grad_low = ref.normed
-    ref.grad_rolled = ref.context_rolled
+    ref.grad_context = ref.product.at[:, : pairs * LANES]
+    ref.grad_three = ref.product.at[:, : 3 * LANES]
+    ref.grad_projected = ref.grad_gate_up
+    ref.acc = ref.grad_product.at[:, : 3 * LANES]
     scatter = Scatter(
         link,
         {
-            "inner": (ref.full, (spans["gate"][0], 2 * main + LANES), spans["gate"][0]),
+            "inner": (ref.grad_inner, (0, 2 * main + LANES), spans["gate"][0]),
             "mlp": (ref.full, spans["mlp"], spans["mlp"][0]),
             "out": (ref.full, spans["out"], spans["out"][0]),
             **{
                 "pair%d" % pair: (
-                    ref.grad_qkv,
-                    (3 * LANES * pair, 3 * LANES),
+                    ref.full,
+                    (spans["gate"][0] + 3 * LANES * pair, 3 * LANES),
                     spans["pair%d" % pair][0],
                 )
                 for pair in range(pairs)
@@ -741,10 +744,7 @@
         unit, scale = norm_parts(ref.tok[at, :])
         ref.unit_one[at, :] = unit
         ref.scale_one[at, :] = jnp.broadcast_to(scale, (128, LANES))
-        here = pl.ds(pl.multiple_of(own_at + at.start, 128), 128)
-        ref.grad_rows[here, :] = ref.cot[at, :].astype(jnp.bfloat16)
-
-    got_grad = link.to_core(ref.grad_rows.at[own, :], ref.grad_rows.at[own, :], 0)
+
     link.send_one("gains")
 
     shift = jnp.int32(0)
@@ -765,6 +765,23 @@
 
     @row_loop(rows, part)
     def _(at):
+        down = source_of(lax.broadcasted_iota(jnp.int32, (part, 1), 0) + at.start)
+        along = lax.broadcasted_iota(jnp.int32, (part, rows), 1)
+        ref.perm[at, :] = jnp.where(down == along, 1.0, 0.0).astype(jnp.bfloat16)
+        down = lax.broadcasted_iota(jnp.int32, (part, rows), 0) + at.start
+        along = source_of(lax.broadcasted_iota(jnp.int32, (1, rows), 1))
+        ref.perm_back[at, :] = jnp.where(down == along, 1.0, 0.0).astype(jnp.bfloat16)
+
+    link.send_two("gains")
+    link.send_one("pair0")
+    link.send_z("pair2")
+
+    @row_loop(half, 128)
+    def _(at):
+        here = pl.ds(pl.multiple_of(own_at + at.start, 128), 128)
+        ref.grad_rows[here, :] = ref.cot[at, :].astype(jnp.bfloat16)
+
+    def table(at):
         place = source_of(lax.broadcasted_iota(jnp.int32, (part, LANES), 0) + at.start)
         start = start_of(place)
         angle = (place - start).astype(jnp.float32) * ref.inverse[...]
@@ -773,20 +790,7 @@
         ref.cosine[at, :] = jnp.cos(angle)
         ref.sine[at, :] = jnp.where(lane % HEAD_DIM < HEAD_DIM // 2, -sine, sine)
 
-    link.send_two("gains")
-    link.send_z("pair2")
-    key_start = start_of(source_of(lax.broadcasted_iota(jnp.int32, (half, 1), 0) + half))
-    query_start = start_of(source_of(lax.broadcasted_iota(jnp.int32, (1, half), 1) + half))
-    ref.bias[...] = jnp.where(key_start == query_start, 0.0, NEGATIVE)
-
-    @row_loop(rows, part)
-    def _(at):
-        down = lax.broadcasted_iota(jnp.int32, (part, rows), 0) + at.start
-        along = lax.broadcasted_iota(jnp.int32, (part, rows), 1)
-        ref.perm[at, :] = jnp.where(source_of(down) == along, 1.0, 0.0).astype(jnp.bfloat16)
-        ref.perm_back[at, :] = jnp.where(source_of(along) == down, 1.0, 0.0).astype(jnp.bfloat16)
-
-    link.send_one("pair0")
+    row_loop(half, part)(table)
     link.arrive("gains")
     slot = lax.broadcasted_iota(jnp.int32, (8, LANES), 0)
     lane = lax.broadcasted_iota(jnp.int32, (8, LANES), 1)
@@ -799,21 +803,30 @@
         ref.normed[here, :] = (ref.unit_one[at, :] * ref.gain[0:1, :]).astype(jnp.bfloat16)
 
     got_normed = link.to_core(ref.normed.at[own, :], ref.normed.at[own, :], 1)
+    got_grad = link.to_core(ref.grad_rows.at[own, :], ref.grad_rows.at[own, :], 0)
     link.send_one("pair1")
+    link.send_z("out")
+
+    @row_loop(half, part)
+    def _(at):
+        table(pl.ds(pl.multiple_of(half + at.start, part), part))
+
+    key_start = start_of(source_of(lax.broadcasted_iota(jnp.int32, (half, 1), 0) + half))
+    query_start = start_of(source_of(lax.broadcasted_iota(jnp.int32, (1, half), 1) + half))
+    ref.bias[...] = jnp.where(key_start == query_start, 0.0, NEGATIVE)
+    got_normed.wait_recv()
     link.send_two("pair0")
-    link.send_z("out")
-    got_normed.wait_recv()
 
     @row_loop(rows, part)
     def _(at):
         ref.rolled[at, :] = dot_nn(ref.perm[at, :], ref.normed[...]).astype(jnp.bfloat16)
 
     link.send_one("pair2")
-    link.send_two("pair1")
     link.send_z("mlp")
 
     def project(pair):
-        link.arrive("pair%d" % pair)
+        if pair:
+            link.arrive("pair%d" % pair)
         cols = slice(pair * LANES, (pair + 1) * LANES)
 
         @row_loop(rows, part)
@@ -829,13 +842,15 @@
             ref.values[at, cols] = three[:, 2 * LANES :].astype(jnp.bfloat16)
             ref.values_t[:, at] = three[:, 2 * LANES :].T.astype(jnp.bfloat16)
 
+    def unit_of(pair, head, first):
+        return (pair * (LANES // HEAD_DIM) + head) * 2 + (0 if first else 1)
+
     def attend(pair, first):
         cols = slice(pair * LANES, (pair + 1) * LANES)
         base = 0 if first else half
 
-        @pl.loop(0, half // part)
-        def _(step):
-            at = pl.ds(pl.multiple_of(base + step * part, part), part)
+        for step in range(half // part):
+            at = pl.ds(base + step * part, part)
             query_pair = ref.queries[at, cols]
             lane = lax.broadcasted_iota(jnp.int32, (part, LANES), 1)
             parts = []
@@ -843,42 +858,49 @@
                 query = jnp.where(lane // HEAD_DIM == head, query_pair, 0)
                 scores = dot_nt(ref.keys[base : base + half, cols], query)
                 if not first:
-                    scores = scores + ref.bias[:, pl.ds(pl.multiple_of(step * part, part), part)]
+                    scores = scores + ref.bias[:, step * part : (step + 1) * part]
                 top = jnp.max(scores, axis=0, keepdims=True)
                 terms = jnp.exp(scores - top)
                 total = jnp.sum(terms, axis=0, keepdims=True)
-                mixed = dot_nn(
-                    ref.values_t[head * HEAD_DIM : (head + 1) * HEAD_DIM, base : base + half],
-                    terms.astype(jnp.bfloat16),
+                probs = (terms * (1.0 / total)).astype(jnp.bfloat16)
+                ref.probs[
+                    unit_of(pair, head, first), :, step * part : (step + 1) * part
+                ] = probs
+                parts.append(
+                    dot_nn(
+                        ref.values_t[head * HEAD_DIM : (head + 1) * HEAD_DIM, base : base + half],
+                        probs,
+                    )
                 )
-                parts.append(mixed * (1.0 / total))
-                ref.lse[pair, head : head + 1, at] = top + jnp.log(total)
             ref.context_rolled[at, cols] = jnp.concatenate(parts, axis=0).T.astype(jnp.bfloat16)
 
+    link.arrive("pair0")
+    link.send_two("pair1")
+    link.send_z("gate")
     project(0)
+    link.send_one("out")
     attend(0, True)
-    link.send_one("out")
     link.send_two("pair2")
-    link.send_z("gate")
+    link.send_z("up")
     attend(0, False)
+    link.send_one("mlp")
     project(1)
+    link.send_two("out")
     attend(1, True)
-    link.send_one("mlp")
-    link.send_two("out")
-    link.send_z("up")
+    link.send_one("gate")
     attend(1, False)
+    link.send_two("mlp")
     project(2)
+    link.send_one("up")
     attend(2, True)
-    link.send_one("gate")
-    link.send_two("mlp")
+    link.send_two("gate")
     attend(2, False)
 
     @row_loop(rows, part)
     def _(at):
         ref.context[at, :] = dot_nn(ref.perm_back[at, :], ref.context_rolled[...]).astype(jnp.bfloat16)
 
-    link.send_one("up")
-    link.send_two("gate")
+    link.send_two("up")
     link.arrive("out")
 
     def pair_sum(product, place, sem, keep):
@@ -912,7 +934,6 @@
         ref.normed_mlp[here, :] = (unit * ref.gain[1:2, :]).astype(jnp.bfloat16)
 
     got_mlp = link.to_core(ref.normed_mlp.at[own, :], ref.normed_mlp.at[own, :], 6)
-    link.send_two("up")
     got_grad.wait_recv()
     link.arrive("mlp")
 
@@ -951,9 +972,6 @@
         ).astype(jnp.bfloat16)
 
     inner = (spans["gate"][0], 2 * main + LANES)
-    got_normed_two = pair_sum(
-        lambda at: dot_nt(ref.grad_gate_up[at, :], weights_at(ref.full, inner)), 1, 3, ref.grad_hidden
-    )
     link.finish()
 
     def weight_grad(left, right, held, first):
@@ -967,8 +985,14 @@
                 2, 2, 2, width // 16, wide
             )
 
-    weight_grad(ref.normed_mlp, ref.grad_gate_up, ref.full, inner[0])
+    weight_grad(ref.normed_mlp, ref.grad_gate_up, ref.grad_inner, 0)
     scatter.one("inner")
+    got_normed_two = pair_sum(
+        lambda at: dot_nt(ref.grad_gate_up[at, :], weights_at(ref.full, inner)), 1, 3, ref.grad_hidden
+    )
+    got_branch = pair_sum(
+        lambda at: dot_nt(ref.product[at, :], weights_at(ref.full, spans["mlp"])), 2, 4, ref.outputs
+    )
     got_normed_two.wait_recv()
     ref.gain_rows[...] = jnp.zeros_like(ref.gain_rows)
 
@@ -985,12 +1009,16 @@
         ref.grad_low[here, :] = grad.astype(jnp.bfloat16)
 
     got_low = link.to_core(ref.grad_low.at[own, :], ref.grad_low.at[own, :], 7)
-    got_branch = pair_sum(
-        lambda at: dot_nt(ref.product[at, :], weights_at(ref.full, spans["mlp"])), 2, 4, ref.outputs
-    )
     weight_grad(ref.grad_rows, ref.product, ref.full, spans["mlp"][0])
     scatter.one("mlp")
-    scatter.two("inner")
+    got_branch.wait_recv()
+
+    @row_loop(half, 128)
+    def _(at):
+        ref.outputs[at, :] = (
+            ref.outputs[at, :] + ref.hidden[at, :] + ref.taken[2, at, :].astype(jnp.float32)
+        )
+
     got_low.wait_recv()
 
     @row_loop(rows, part)
@@ -1005,15 +1033,7 @@
 
     weight_grad(ref.grad_low, ref.context, ref.full, spans["out"][0])
     scatter.one("out")
-    scatter.two("mlp")
-    scatter.three("inner")
-    got_branch.wait_recv()
-
-    @row_loop(half, 128)
-    def _(at):
-        ref.outputs[at, :] = (
-            ref.outputs[at, :] + ref.hidden[at, :] + ref.taken[2, at, :].astype(jnp.float32)
-        )
+    scatter.two("inner")
 
     def pull(pair, first):
         cols = slice(pair * LANES, (pair + 1) * LANES)
@@ -1025,25 +1045,26 @@
             at = pl.ds(pl.multiple_of(base + at.start, part), part)
             ref.keys_t[:, at] = ref.keys[at, cols].astype(jnp.float32).T.astype(jnp.bfloat16)
 
-        @pl.loop(0, half // part)
-        def _(step):
-            at = pl.ds(pl.multiple_of(base + step * part, part), part)
+        for step in range(half // part):
+            at = pl.ds(base + step * part, part)
             lane = lax.broadcasted_iota(jnp.int32, (part, LANES), 1)
             query_pair = ref.queries[at, cols]
             grad_pair = ref.grad_rolled[at, cols]
+            product = grad_pair.astype(jnp.float32) * ref.context_rolled[at, cols].astype(jnp.float32)
+            product = product.T
             parts, all_probs, all_grads, all_queries, all_pulls = [], [], [], [], []
             for head in range(LANES // HEAD_DIM):
                 query = jnp.where(lane // HEAD_DIM == head, query_pair, 0)
                 grad = jnp.where(lane // HEAD_DIM == head, grad_pair, 0)
-                scores = dot_nt(ref.keys[span, cols], query)
-                if not first:
-                    scores = scores + ref.bias[:, pl.ds(pl.multiple_of(step * part, part), part)]
-                probs = jnp.exp(scores - ref.lse[pair, head : head + 1, at])
+                probs = ref.probs[
+                    unit_of(pair, head, first), :, step * part : (step + 1) * part
+                ]
                 grad_probs = dot_nt(ref.values[span, cols], grad)
-                weighted = probs * grad_probs
-                drop = jnp.sum(weighted, axis=0, keepdims=True)
-                pulled = (weighted - probs * drop).astype(jnp.bfloat16)
-                all_probs.append(probs.astype(jnp.bfloat16))
+                drop = jnp.sum(
+                    product[head * HEAD_DIM : (head + 1) * HEAD_DIM], axis=0, keepdims=True
+                )
+                pulled = (probs.astype(jnp.float32) * (grad_probs - drop)).astype(jnp.bfloat16)
+                all_probs.append(probs)
                 all_grads.append(grad)
                 all_queries.append(query)
                 all_pulls.append(pulled)
@@ -1057,13 +1078,10 @@
                 jnp.concatenate(all_pulls, axis=1), jnp.concatenate(all_queries, axis=0)
             )
 
-            @pl.when(step == 0)
-            def _():
+            if step == 0:
                 ref.acc[span, LANES : 2 * LANES] = grad_keys
                 ref.acc[span, 2 * LANES :] = grad_values
-
-            @pl.when(step > 0)
-            def _():
+            else:
                 ref.acc[span, LANES : 2 * LANES] += grad_keys
                 ref.acc[span, 2 * LANES :] += grad_values
 
@@ -1082,7 +1100,7 @@
             ref.grad_three[at, LANES : 2 * LANES] = grad_key.astype(jnp.bfloat16)
             ref.grad_three[at, 2 * LANES :] = ref.acc[at, 2 * LANES :].astype(jnp.bfloat16)
 
-        weight_grad(ref.rolled, ref.grad_three, ref.grad_qkv, first)
+        weight_grad(ref.rolled, ref.grad_three, ref.full, spans["gate"][0] + first)
         scatter.one("pair%d" % pair)
 
         @row_loop(rows, part)
@@ -1092,32 +1110,30 @@
             ).astype(jnp.bfloat16)
 
     pull(0, True)
+    scatter.two("mlp")
+    pull(0, False)
+    unproject(0)
+    scatter.three("inner")
+    pull(1, True)
     scatter.two("out")
+    pull(1, False)
     scatter.three("mlp")
-    pull(0, False)
+    unproject(1)
+    pull(2, True)
+    scatter.two("pair0")
+    scatter.three("out")
     scatter.four("inner")
-    unproject(0)
-    scatter.three("out")
-    pull(1, True)
-    scatter.two("pair0")
+    pull(2, False)
+    unproject(2)
+    scatter.three("pair0")
+    scatter.two("pair1")
     scatter.four("mlp")
-    pull(1, False)
-    scatter.three("pair0")
-    unproject(1)
-    scatter.four("out")
-    pull(2, True)
-    scatter.two("pair1")
-    scatter.four("pair0")
-    pull(2, False)
-    scatter.three("pair1")
-    unproject(2)
     qkv_span = (spans["pair0"][0], 3 * pairs * LANES)
     got_one = pair_sum(
         lambda at: dot_nt(ref.grad_projected[at, :], weights_at(ref.full, qkv_span)),
         0, 5, ref.grad_tokens,
     )
-    scatter.two("pair2")
-    scatter.four("pair1")
+    scatter.three("pair1")
     got_one.wait_recv()
 
     @row_loop(half, 128)
@@ -1130,7 +1146,8 @@
         )
 
     got_gain = link.to_core(ref.gain_rows, ref.gain_other, 8)
-    scatter.three("pair2")
+    scatter.two("pair2")
+    scatter.four("out")
     got_gain.wait_recv()
     gain_rows = ref.gain_rows[...] + ref.gain_other[...]
     high = gain_rows.astype(jnp.bfloat16)
@@ -1141,9 +1158,12 @@
     columns = dot_tn(jnp.concatenate([high, rest], axis=0), pick).astype(jnp.bfloat16)
     ref.full[:, :, :, :, 0:LANES] = columns.reshape(4, 2, 2, width // 16, LANES)
     scatter.one("gains")
+    scatter.four("pair0")
+    scatter.three("pair2")
+    scatter.two("gains")
+    scatter.four("pair1")
+    scatter.three("gains")
     scatter.four("pair2")
-    scatter.two("gains")
-    scatter.three("gains")
     scatter.four("gains")
     link.finish()
 
@@ -1169,7 +1189,7 @@
     chunk_count = 1 + pairs + 4
     kept = dict(
         full=((4, 2, 2, height, total), low),
-        grad_qkv=((4, 2, 2, height, 3 * width_here), low),
+        grad_inner=((4, 2, 2, height, 2 * main + LANES), low),
         low_one=((2, 2, height, total), low),
         high_one=((2, 2, height, total), low),
         low_two=((2, height, total), low),
@@ -1189,11 +1209,8 @@
         values=((rows, width_here), low),
         context=((rows, width_here), low),
         context_rolled=((rows, width_here), low),
-        grad_context=((rows, width_here), low),
-        grad_three=((rows, 3 * LANES), low),
-        grad_projected=((rows, 3 * width_here), low),
-        acc=((rows, 3 * LANES), wide),
-        lse=((pairs, LANES // HEAD_DIM, rows), wide),
+        probs=((2 * width_here // HEAD_DIM, half, half), low),
+        grad_rolled=((rows, width_here), low),
         product=((rows, main + LANES), low),
         grad_gate_up=((rows, 2 * main + LANES), low),
         grad_product=((rows, main + LANES), wide),

time: 168 us -> 148 us (0.88)
  Pallas kernels: 153 us -> 132 us
    pallas_call x1, Pallas kernels: 153 us -> 132 us  [call_layer(): pl.pallas_call(functools.partial(layer_kernel, names, spans), out_shape=[...]
where the time goes in v2:
time: 148 us; the launch traced here: 147 us
  Pallas kernels  132 us (89%)
  local copies, waits for them, and re-layouts  13.5 us (9%)
    pallas_call x1, Pallas kernels, call_layer(): pl.pallas_call(functools.partial(layer_kernel, names, spans), out_shape=[...  132 us
    unnamed x13, local copies, waits for them, and re-layouts  3.95 us

profile of v2, /device:TPU:0, one launch (start us, length us, event | category | flops | bytes accessed | tf_op | source)
XLA Modules:
  0.0 147.2 jit_solution(10616276995940123948)
XLA Ops:
  0.6 0.0 copy-start.4
  0.6 0.0 copy-start.3
  0.7 0.8 copy.31
  1.4 0.8 copy.32
  2.2 0.9 reshape.35
  3.1 0.1 copy.26
  3.3 0.1 reshape.36
  3.4 1.1 fusion.3
  4.5 0.9 fusion.2
  5.4 0.0 copy-done.4
  5.4 0.0 copy-done.3
  5.4 0.8 concatenate.9.refs_1_
  6.3 0.6 broadcast_in_dim_tile.3.refs_4_
  6.9 132.2 %shard_map.152 = (f32[512,768]{1,0:T(8,128)}, f32[512,768]{1,0:T(8,128)}, f32[48,3456]{1,0:T(8,128)}) custom-call(s32[1,16]{1,0:T(1,128)} %refs_0_.1, bf16[48,3456]{1,0:T(8,128)(2,1)} %concatenate.9.refs_1_, f32[512,768]{1,0:T(8,128)} %refs_2_.1, f32[512,768]{1,0:T(8,128)} %refs_3_.1, f32[1,128]{1,0:T(1,128)} %broadcast_in_dim_tile.3.refs_4_), custom_call_target="tpu_custom_call" | custom-call | flops 12000000000 | bytes 30000000 | tf_op jit(solution)/shard_map/pallas_call | solution.py:1239
  139.1 0.0 copy-start.2
  139.1 1.0 slice.54
  140.1 0.1 reshape.37
  140.2 0.1 copy.33
  140.3 0.0 copy-start.1
  140.3 0.8 reshape.38
  141.1 0.0 copy-done.2
  141.1 0.6 slice_bitcast_fusion.1
  141.8 0.1 fusion.1
  141.9 0.8 copy.34
  142.7 0.7 slice_bitcast_fusion
  143.4 0.7 add_reduce_fusion
  144.1 0.0 copy-done.1
  144.1 0.0 copy-start
  144.1 1.1 copy.45
  145.2 0.8 copy-done
  146.1 1.1 copy.46
  (10 shorter events, 0.1 us)
Async XLA Ops:
  0.6 4.8 %copy-start.4 = (bf16[384,48]{0,1:T(8,128)(2,1)S(1)}, bf16[384,48]{0,1:T(8,128)(2,1)}, u32[]{:S(2)}) copy-start(bf16[384,48]{0,1:T(8,128)(2,1)} %param.12) | copy-start | bytes 110596
  0.6 4.8 %copy-start.3 = (bf16[576,48]{0,1:T(8,128)(2,1)S(1)}, bf16[576,48]{0,1:T(8,128)(2,1)}, u32[]{:S(2)}) copy-start(bf16[576,48]{0,1:T(8,128)(2,1)} %param.14) | copy-start | bytes 165892
  139.1 2.0 %copy-start.2 = (f32[48,3456]{1,0:T(8,128)S(1)}, f32[48,3456]{1,0:T(8,128)}, u32[]{:S(2)}) copy-start(f32[48,3456]{1,0:T(8,128)} %get-tuple-element.13) | copy-start | bytes 1990660
  140.3 3.8 %copy-start.1 = (f32[512,768]{1,0:T(8,128)S(1)}, f32[512,768]{1,0:T(8,128)}, u32[]{:S(2)}) copy-start(f32[512,768]{1,0:T(8,128)} %get-tuple-element.52) | copy-start | bytes 4718596
  144.1 2.0 %copy-start = (f32[512,768]{1,0:T(8,128)S(1)}, f32[512,768]{1,0:T(8,128)}, u32[]{:S(2)}) copy-start(f32[512,768]{1,0:T(8,128)} %get-tuple-element.53) | copy-start | bytes 4718596

commit v3 on v2

--- a/solution.py
+++ b/solution.py
@@ -4,6 +4,7 @@
 
 import jax
 import jax.numpy as jnp
+import numpy as np
 from jax import lax
 from jax.experimental import pallas as pl
 from jax.experimental.pallas import tpu as pltpu
@@ -467,30 +468,37 @@
     return at
 
 
-def pack_shards(w_qkv, w_attn_out, w_in, w_mlp_out, gain_attn, gain_mlp):
-    height, _, width_here = w_qkv.shape
-    hidden_here = w_in.shape[2]
-    main = hidden_here // LANES * LANES
-    pairs = width_here // LANES
-    gains = jnp.concatenate(
-        [gain_attn[:, None], gain_mlp[:, None], jnp.zeros((height, LANES - 2), jnp.bfloat16)], axis=1
-    )
-    by_pair = w_qkv.reshape(height, 3, pairs, LANES).transpose(0, 2, 1, 3)
-    short = main + LANES - hidden_here
-    return jnp.concatenate(
-        [
-            gains,
-            by_pair.reshape(height, 3 * width_here),
-            w_attn_out.T,
-            w_mlp_out.T,
-            jnp.zeros((height, short), jnp.bfloat16),
-            w_in[:, 0, :main],
-            w_in[:, 1, :main],
-            w_in[:, 0, main:],
-            w_in[:, 1, main:],
-        ],
-        axis=1,
-    )
+def pack_shards(ref, spans):
+    height = ref.w_attn_out.shape[0]
+    main = spans["gate"][1]
+    hidden_here = ref.w_in.shape[1] // 2
+    pairs = spans["out"][1] // LANES
+    wide = jnp.float32
+    down = lax.broadcasted_iota(jnp.int32, (height, height), 0)
+    along = lax.broadcasted_iota(jnp.int32, (height, height), 1)
+    lane = lax.broadcasted_iota(jnp.int32, (height, LANES), 1)
+    gains = jnp.zeros((height, LANES), wide)
+    for place, row in enumerate((ref.gain_one, ref.gain_two)):
+        column = jnp.sum(jnp.where(down == along, row[...].astype(wide), 0.0), axis=1, keepdims=True)
+        gains = jnp.where(lane == place, column, gains)
+    pieces = [gains.astype(jnp.bfloat16)]
+    for pair in range(pairs):
+        for kind in range(3):
+            pieces.append(ref.w_qkv[kind, :, pair * LANES : (pair + 1) * LANES])
+    tail = jnp.concatenate(
+        [ref.w_in[:, main:hidden_here], ref.w_in[:, hidden_here + main :]], axis=1
+    )
+    mlp = jnp.concatenate(
+        [ref.w_mlp_out[...], jnp.zeros((height, main + LANES - hidden_here), jnp.bfloat16)], axis=1
+    )
+    pieces += [
+        ref.w_attn_out[...],
+        mlp,
+        ref.w_in[:, :main],
+        ref.w_in[:, hidden_here : hidden_here + main],
+        tail,
+    ]
+    return pieces
 
 
 class Links:
@@ -676,7 +684,7 @@
         total = held[link.z, link.y, link.x, :, cols].astype(jnp.float32)
         for step in range(3):
             total = total + ref.far_sum[step, :, to].astype(jnp.float32)
-        ref.sums[:, to] = total
+        return total
 
 
 def weights_at(full, span):
@@ -697,6 +705,10 @@
     ref = types.SimpleNamespace(**dict(zip(names, refs)))
     half, width = ref.tok.shape
     rows = 2 * half
+    fetch_tok = pltpu.make_async_copy(ref.tokens, ref.tok, ref.fetch.at[0])
+    fetch_cot = pltpu.make_async_copy(ref.cotangent, ref.cot, ref.fetch.at[1])
+    fetch_tok.start()
+    fetch_cot.start()
     pairs = (spans["out"][1]) // LANES
     main = spans["gate"][1]
     chunk_names = ["gains"] + ["pair%d" % pair for pair in range(pairs)] + ["out", "mlp"]
@@ -733,11 +745,17 @@
         },
     )
 
+    place = 0
+    for piece in pack_shards(ref, spans):
+        wide = piece.shape[1]
+        ref.full[link.z, link.y, link.x, :, place : place + wide] = piece
+        place += wide
     link.enter()
-    ref.full[link.z, link.y, link.x] = ref.pack[...]
     link.send_z("gains")
     link.send_z("pair0")
     link.send_z("pair1")
+
+    fetch_tok.wait()
 
     @row_loop(half, 128)
     def _(at):
@@ -775,6 +793,8 @@
     link.send_two("gains")
     link.send_one("pair0")
     link.send_z("pair2")
+
+    fetch_cot.wait()
 
     @row_loop(half, 128)
     def _(at):
@@ -1034,6 +1054,29 @@
     weight_grad(ref.grad_low, ref.context, ref.full, spans["out"][0])
     scatter.one("out")
     scatter.two("inner")
+
+    def settle(name):
+        total = scatter.four(name)
+        hidden_here = ref.grad_mlp_out.shape[1]
+        short = hidden_here - main
+        if name == "inner":
+            ref.grad_in[:, :main] = total[:, :main]
+            ref.grad_in[:, main:hidden_here] = total[:, 2 * main : 2 * main + short]
+            ref.grad_in[:, hidden_here : hidden_here + main] = total[:, main : 2 * main]
+            ref.grad_in[:, hidden_here + main :] = total[:, 2 * main + short :]
+        elif name == "mlp":
+            ref.grad_mlp_out[...] = total[:, :hidden_here]
+        elif name == "out":
+            ref.grad_attn_out[...] = total
+        elif name == "gains":
+            turned = total.T
+            ref.gains[...] = turned[0:2, :] + turned[8:10, :]
+        else:
+            pair = int(name[4:])
+            for kind in range(3):
+                ref.grad_qkv[kind, :, pair * LANES : (pair + 1) * LANES] = total[
+                    :, kind * LANES : (kind + 1) * LANES
+                ]
 
     def pull(pair, first):
         cols = slice(pair * LANES, (pair + 1) * LANES)
@@ -1122,12 +1165,12 @@
     pull(2, True)
     scatter.two("pair0")
     scatter.three("out")
-    scatter.four("inner")
+    settle("inner")
     pull(2, False)
     unproject(2)
     scatter.three("pair0")
     scatter.two("pair1")
-    scatter.four("mlp")
+    settle("mlp")
     qkv_span = (spans["pair0"][0], 3 * pairs * LANES)
     got_one = pair_sum(
         lambda at: dot_nt(ref.grad_projected[at, :], weights_at(ref.full, qkv_span)),
@@ -1147,7 +1190,7 @@
 
     got_gain = link.to_core(ref.gain_rows, ref.gain_other, 8)
     scatter.two("pair2")
-    scatter.four("out")
+    settle("out")
     got_gain.wait_recv()
     gain_rows = ref.gain_rows[...] + ref.gain_other[...]
     high = gain_rows.astype(jnp.bfloat16)
@@ -1158,33 +1201,37 @@
     columns = dot_tn(jnp.concatenate([high, rest], axis=0), pick).astype(jnp.bfloat16)
     ref.full[:, :, :, :, 0:LANES] = columns.reshape(4, 2, 2, width // 16, LANES)
     scatter.one("gains")
-    scatter.four("pair0")
+    settle("pair0")
     scatter.three("pair2")
     scatter.two("gains")
-    scatter.four("pair1")
+    settle("pair1")
     scatter.three("gains")
-    scatter.four("pair2")
-    scatter.four("gains")
+    settle("pair2")
+    settle("gains")
     link.finish()
 
 
-def call_layer(pack, tokens, cotangent, offsets, spans):
+def call_layer(shards_here, tokens, cotangent, offsets, spans):
     half, width = tokens.shape
     rows = 2 * half
-    height, total = pack.shape
+    height = shards_here["w_attn_out"].shape[0]
+    total = spans["total"][1]
     width_here = spans["out"][1]
+    hidden_here = shards_here["w_mlp_out"].shape[1]
     pairs = width_here // LANES
     main = spans["gate"][1]
     half_dim = HEAD_DIM // 2
-    inverse = jnp.power(
-        jnp.float32(ROPE_BASE), -2.0 * jnp.arange(half_dim, dtype=jnp.float32) / HEAD_DIM
-    )
-    inverse = jnp.tile(inverse, LANES // half_dim)[None, :]
+    inverse = np.power(ROPE_BASE, -2.0 * np.arange(half_dim) / HEAD_DIM).astype(np.float32)
+    inverse = jnp.asarray(np.tile(inverse, LANES // half_dim)[None, :])
     low, wide = jnp.bfloat16, jnp.float32
     outs = dict(
         outputs=((half, width), wide),
         grad_tokens=((half, width), wide),
-        sums=((height, total), wide),
+        grad_qkv=((3, height, width_here), wide),
+        grad_attn_out=((height, width_here), wide),
+        grad_in=((height, 2 * hidden_here), wide),
+        grad_mlp_out=((height, hidden_here), wide),
+        gains=((2, height), wide),
     )
     chunk_count = 1 + pairs + 4
     kept = dict(
@@ -1228,18 +1275,20 @@
         gain_rows=((8, width), wide),
         gain_other=((8, width), wide),
     )
+    kept.update(tok=((half, width), wide), cot=((half, width), wide))
     scratch = {name: pltpu.VMEM(*entry) for name, entry in kept.items()}
+    scratch["fetch"] = pltpu.SemaphoreType.DMA((2,))
     for name, count in (
         ("far", 3 * chunk_count), ("near", 4 * chunk_count), ("core", 9), ("sum", 7 * (pairs + 4)),
     ):
         scratch[name + "_out"] = pltpu.SemaphoreType.DMA((count,))
         scratch[name + "_in"] = pltpu.SemaphoreType.DMA((count,))
-    names = ["offsets", "pack", "tok", "cot", "inverse"] + list(outs) + list(scratch)
+    names = ["offsets", "tokens", "cotangent", "inverse"] + list(shards_here) + list(outs) + list(scratch)
     vmem = pl.BlockSpec(memory_space=pltpu.VMEM)
     results = pl.pallas_call(
         functools.partial(layer_kernel, names, spans),
         out_shape=[jax.ShapeDtypeStruct(*entry) for entry in outs.values()],
-        in_specs=[pl.BlockSpec(memory_space=pltpu.SMEM)] + [vmem] * 4,
+        in_specs=[pl.BlockSpec(memory_space=pltpu.SMEM)] + [pl.BlockSpec(memory_space=pl.ANY)] * 2 + [vmem] * (1 + len(shards_here)),
         out_specs=[vmem] * len(outs),
         scratch_shapes=list(scratch.values()),
         compiler_params=pltpu.CompilerParams(
@@ -1248,37 +1297,33 @@
         cost_estimate=pl.CostEstimate(
             flops=12 * 10**9, bytes_accessed=30 * 10**6, transcendentals=10**7
         ),
-    )(offsets, pack, tokens, cotangent, inverse)
+    )(offsets, tokens, cotangent, inverse, *shards_here.values())
     return types.SimpleNamespace(**dict(zip(outs, results)))
 
 
 def fast_shards(tokens, offsets, w_qkv, w_attn_out, w_in, w_mlp_out, gain_attn, gain_mlp, cotangent):
     half = tokens.shape[0]
-    rows = 2 * half
     height, _, width_here = w_qkv.shape
     hidden_here = w_in.shape[2]
-    pairs = width_here // LANES
-    main = hidden_here // LANES * LANES
     spans = fast_columns(width_here, hidden_here)
-    pack = pack_shards(w_qkv, w_attn_out, w_in, w_mlp_out, gain_attn, gain_mlp)
-    f = call_layer(pack, tokens, cotangent, offsets, spans)
-    pick = lambda name: f.sums[:, spans[name][0] : spans[name][0] + spans[name][1]]
-    at = spans["pair0"][0]
-    tail = pick("tail")
-    gate = jnp.concatenate([pick("gate"), tail[:, : hidden_here - main]], axis=1)
-    up = jnp.concatenate([pick("up"), tail[:, hidden_here - main :]], axis=1)
+    shards_here = dict(
+        w_qkv=w_qkv.transpose(1, 0, 2),
+        w_attn_out=w_attn_out.T,
+        w_in=w_in.reshape(height, -1),
+        w_mlp_out=w_mlp_out.T,
+        gain_one=gain_attn[None, :],
+        gain_two=gain_mlp[None, :],
+    )
+    f = call_layer(shards_here, tokens, cotangent, offsets, spans)
     return (
         f.outputs,
         f.grad_tokens,
-        f.sums[:, at : at + 3 * width_here]
-        .reshape(height, pairs, 3, LANES)
-        .transpose(0, 2, 1, 3)
-        .reshape(height, 3, width_here),
-        pick("out").T,
-        jnp.stack([gate, up], axis=1),
-        pick("mlp")[:, :hidden_here].T,
-        f.sums[:, 0] + f.sums[:, 8],
-        f.sums[:, 1] + f.sums[:, 9],
+        f.grad_qkv.transpose(1, 0, 2),
+        f.grad_attn_out.T,
+        f.grad_in.reshape(height, 2, hidden_here),
+        f.grad_mlp_out.T,
+        f.gains[0],
+        f.gains[1],
     )
 
 

time: 148 us -> 143 us (0.966)
  local copies, waits for them, and re-layouts: 13.5 us -> 10.7 us
    slice x5 -> x0, local copies, waits for them, and re-layouts: 3.11 us -> none  [the longest x1 1.14 us: pack_shards(): w_in[:, 1, :main]]
    unnamed x13, local copies, waits for them, and re-layouts: 3.95 us -> 5.9 us
    reshape x4 -> x2, local copies, waits for them, and re-layouts: 1.92 us -> 3.52 us  [the longest x1 1.83 us: fast_shards(): f.grad_in.reshape(height, 2, hidden_here)]
    broadcast_in_dim x4 -> x0, local copies, waits for them, and re-layouts: 1.55 us -> none  [the longest x1 0.78 us: pack_shards(): gain_attn[:, None]]
    transpose x4 -> x0, local copies, waits for them, and re-layouts: 1.49 us -> none  [the longest x1 0.66 us: fast_shards(): pick('mlp')[:, :hidden_here]]
where the time goes in v3:
time: 143 us
  Pallas kernels  131 us (92%)
  local copies, waits for them, and re-layouts  10.7 us (7%)
    pallas_call x1, Pallas kernels, call_layer(): pl.pallas_call(functools.partial(layer_kernel, names, spans), out_shape=[...  131 us
    unnamed x13, local copies, waits for them, and re-layouts  5.9 us

profile of v3, /device:TPU:0, one launch (start us, length us, event | category | flops | bytes accessed | tf_op | source)
XLA Modules:
  0.0 142.7 jit_solution(4093574303913007141)
XLA Ops:
  0.6 1.7 %reshape.22.refs_6_ = bf16[48,1152]{1,0:T(8,128)(2,1)} reshape(bf16[48,2,576]{2,1,0:T(2,128)(2,1)} %param.14) | data formatting | bytes 221184 | tf_op jit(solution)/shard_map/reshape | solution.py:1312
  2.3 131.4 %shard_map.161 = (f32[512,768]{1,0:T(8,128)}, f32[512,768]{1,0:T(8,128)}, f32[3,48,384]{2,1,0:T(8,128)}, f32[48,384]{1,0:T(8,128)}, f32[48,1152]{1,0:T(8,128)}, /*index=5*/f32[48,576]{1,0:T(8,128)}, f32[2,48]{1,0:T(2,128)}) custom-call(s32[1,16]{1,0:T(1,128)} %refs_0_.1, f32[512,768]{1,0:T(8,128)} %refs_1_.1, f32[512,768]{1,0:T(8,128)} %refs_2_.1, ...), custom_call_target="tpu_custom_call" | custom-call | flops 12000000000 | bytes 30000000 | tf_op jit(solution)/shard_map/pallas_call | solution.py:1288
  133.7 1.3 slice_bitcast_fusion
  135.0 1.8 %reshape.23 = f32[48,2,576]{2,1,0:T(2,128)} reshape(f32[48,1152]{1,0:T(8,128)} %get-tuple-element.19) | data formatting | bytes 442368 | tf_op jit(solution)/shard_map/reshape | solution.py:1323
  136.8 0.0 copy-start
  136.8 2.8 %copy.23 = f32[512,768]{1,0:T(8,128)} copy(f32[512,768]{1,0:T(8,128)} %get-tuple-element.32) | data formatting | bytes 3145728
  139.6 0.0 copy-done
  139.6 0.0 copy-start.1
  139.6 0.0 copy-start.3
  139.6 0.0 copy-start.2
  139.6 1.1 copy.24
  140.7 0.0 copy-done.1
  140.7 0.7 copy.25
  141.4 0.0 copy-done.3
  141.4 0.6 copy.26
  142.1 0.0 copy-done.2
  142.1 0.6 copy.27
Async XLA Ops:
  136.8 2.8 %copy-start = (f32[512,768]{1,0:T(8,128)S(1)}, f32[512,768]{1,0:T(8,128)}, u32[]{:S(2)}) copy-start(f32[512,768]{1,0:T(8,128)} %get-tuple-element.33) | copy-start | bytes 4718596
  139.6 1.2 copy-start.1
  139.6 1.8 %copy-start.3 = (f32[48,384]{1,0:T(8,128)S(1)}, f32[48,384]{1,0:T(8,128)}, u32[]{:S(2)}) copy-start(f32[48,384]{1,0:T(8,128)} %get-tuple-element.18) | copy-start | bytes 221188
  139.6 2.5 %copy-start.2 = (f32[48,576]{1,0:T(8,128)S(1)}, f32[48,576]{1,0:T(8,128)}, u32[]{:S(2)}) copy-start(f32[48,576]{1,0:T(8,128)} %get-tuple-element.20) | copy-start | bytes 331780

commit v4 on v3

--- a/solution.py
+++ b/solution.py
@@ -1060,10 +1060,10 @@
         hidden_here = ref.grad_mlp_out.shape[1]
         short = hidden_here - main
         if name == "inner":
-            ref.grad_in[:, :main] = total[:, :main]
-            ref.grad_in[:, main:hidden_here] = total[:, 2 * main : 2 * main + short]
-            ref.grad_in[:, hidden_here : hidden_here + main] = total[:, main : 2 * main]
-            ref.grad_in[:, hidden_here + main :] = total[:, 2 * main + short :]
+            ref.grad_gate[:, :main] = total[:, :main]
+            ref.grad_gate[:, main:] = total[:, 2 * main : 2 * main + short]
+            ref.grad_up[:, :main] = total[:, main : 2 * main]
+            ref.grad_up[:, main:] = total[:, 2 * main + short :]
         elif name == "mlp":
             ref.grad_mlp_out[...] = total[:, :hidden_here]
         elif name == "out":
@@ -1229,7 +1229,8 @@
         grad_tokens=((half, width), wide),
         grad_qkv=((3, height, width_here), wide),
         grad_attn_out=((height, width_here), wide),
-        grad_in=((height, 2 * hidden_here), wide),
+        grad_gate=((height, hidden_here), wide),
+        grad_up=((height, hidden_here), wide),
         grad_mlp_out=((height, hidden_here), wide),
         gains=((2, height), wide),
     )
@@ -1320,7 +1321,7 @@
         f.grad_tokens,
         f.grad_qkv.transpose(1, 0, 2),
         f.grad_attn_out.T,
-        f.grad_in.reshape(height, 2, hidden_here),
+        jnp.stack([f.grad_gate, f.grad_up], axis=1),
         f.grad_mlp_out.T,
         f.gains[0],
         f.gains[1],

time: 143 us -> 143 us (level)
    reshape x1 -> x0, local copies, waits for them, and re-layouts: 1.83 us -> none  [fast_shards(): f.grad_in.reshape(height, 2, hidden_here)]
    unnamed x13 -> x14, local copies, waits for them, and re-layouts: 5.9 us -> 6.72 us
where the time goes in v4:
time: 143 us
  Pallas kernels  131 us (92%)
  local copies, waits for them, and re-layouts  9.63 us (7%)
    pallas_call x1, Pallas kernels, call_layer(): pl.pallas_call(functools.partial(layer_kernel, names, spans), out_shape=[...  131 us
    unnamed x14, local copies, waits for them, and re-layouts  6.72 us

profile of v4, /device:TPU:0, one launch (start us, length us, event | category | flops | bytes accessed | tf_op | source)
XLA Modules:
  0.0 142.6 jit_solution(10692352768338883078)
XLA Ops:
  0.6 1.7 %reshape.19.refs_6_ = bf16[48,1152]{1,0:T(8,128)(2,1)} reshape(bf16[48,2,576]{2,1,0:T(2,128)(2,1)} %param.14) | data formatting | bytes 221184 | tf_op jit(solution)/shard_map/reshape | solution.py:1313
  2.3 131.4 %shard_map.161 = (f32[512,768]{1,0:T(8,128)}, f32[512,768]{1,0:T(8,128)}, f32[3,48,384]{2,1,0:T(8,128)}, f32[48,384]{1,0:T(8,128)}, f32[48,576]{1,0:T(8,128)}, /...) custom-call(s32[1,16]{1,0:T(1,128)} %refs_0_.1, f32[512,768]{1,0:T(8,128)} %refs_1_.1, f32[512,768]{1,0:T(8,128)} %refs_2_.1, ...), custom_call_target="tpu_custom_call" | custom-call | flops 12000000000 | bytes 30000000 | tf_op jit(solution)/shard_map/pallas_call | solution.py:1289
  133.7 1.2 slice_bitcast_fusion
  134.9 1.0 pad_maximum_fusion
  135.9 0.8 copy.18
  136.7 0.0 copy-start
  136.7 2.8 %copy.24 = f32[512,768]{1,0:T(8,128)} copy(f32[512,768]{1,0:T(8,128)} %get-tuple-element.42) | data formatting | bytes 3145728
  139.5 0.0 copy-done
  139.5 0.0 copy-start.1
  139.5 0.0 copy-start.3
  139.5 0.0 copy-start.2
  139.5 1.1 copy.25
  140.7 0.0 copy-done.1
  140.7 0.7 copy.26
  141.3 0.0 copy-done.3
  141.3 0.6 copy.27
  142.0 0.0 copy-done.2
  142.0 0.6 copy.28
Async XLA Ops:
  136.7 2.8 %copy-start = (f32[512,768]{1,0:T(8,128)S(1)}, f32[512,768]{1,0:T(8,128)}, u32[]{:S(2)}) copy-start(f32[512,768]{1,0:T(8,128)} %get-tuple-element.43) | copy-start | bytes 4718596
  139.5 1.2 copy-start.1
  139.5 1.8 %copy-start.3 = (f32[48,384]{1,0:T(8,128)S(1)}, f32[48,384]{1,0:T(8,128)}, u32[]{:S(2)}) copy-start(f32[48,384]{1,0:T(8,128)} %get-tuple-element.19) | copy-start | bytes 221188
  139.5 2.5 %copy-start.2 = (f32[48,576]{1,0:T(8,128)S(1)}, f32[48,576]{1,0:T(8,128)}, u32[]{:S(2)}) copy-start(f32[48,576]{1,0:T(8,128)} %get-tuple-element.22) | copy-start | bytes 331780

commit v5 on v4

--- a/solution.py
+++ b/solution.py
@@ -1170,7 +1170,6 @@
     unproject(2)
     scatter.three("pair0")
     scatter.two("pair1")
-    settle("mlp")
     qkv_span = (spans["pair0"][0], 3 * pairs * LANES)
     got_one = pair_sum(
         lambda at: dot_nt(ref.grad_projected[at, :], weights_at(ref.full, qkv_span)),
@@ -1182,15 +1181,18 @@
     @row_loop(half, 128)
     def _(at):
         incoming = ref.grad_tokens[at, :] + ref.taken[0, at, :].astype(jnp.float32)
-        unit = ref.unit_one[at, :]
-        ref.gain_rows[0:1, :] += jnp.sum(incoming * unit, axis=0, keepdims=True)
-        ref.grad_tokens[at, :] = ref.grad_hidden[at, :] + norm_backward(
-            incoming, ref.gain[0:1, :], unit, ref.scale_one[at, 0:1]
-        )
+        ref.grad_tokens[at, :] = incoming
+        ref.gain_rows[0:1, :] += jnp.sum(incoming * ref.unit_one[at, :], axis=0, keepdims=True)
 
     got_gain = link.to_core(ref.gain_rows, ref.gain_other, 8)
     scatter.two("pair2")
-    settle("out")
+
+    @row_loop(half, 128)
+    def _(at):
+        ref.grad_tokens[at, :] = ref.grad_hidden[at, :] + norm_backward(
+            ref.grad_tokens[at, :], ref.gain[0:1, :], ref.unit_one[at, :], ref.scale_one[at, 0:1]
+        )
+
     got_gain.wait_recv()
     gain_rows = ref.gain_rows[...] + ref.gain_other[...]
     high = gain_rows.astype(jnp.bfloat16)
@@ -1201,11 +1203,13 @@
     columns = dot_tn(jnp.concatenate([high, rest], axis=0), pick).astype(jnp.bfloat16)
     ref.full[:, :, :, :, 0:LANES] = columns.reshape(4, 2, 2, width // 16, LANES)
     scatter.one("gains")
+    scatter.three("pair2")
+    settle("out")
+    settle("mlp")
+    scatter.two("gains")
     settle("pair0")
-    scatter.three("pair2")
-    scatter.two("gains")
+    scatter.three("gains")
     settle("pair1")
-    scatter.three("gains")
     settle("pair2")
     settle("gains")
     link.finish()

time: 143 us -> 142 us (level)
  no operation moved by 1% of the time
where the time goes in v5:
time: 142 us
  Pallas kernels  131 us (92%)
  local copies, waits for them, and re-layouts  9.63 us (7%)
    pallas_call x1, Pallas kernels, call_layer(): pl.pallas_call(functools.partial(layer_kernel, names, spans), out_shape=[...  131 us
    unnamed x14, local copies, waits for them, and re-layouts  6.72 us

profile of v5, /device:TPU:0, one launch (start us, length us, event | category | flops | bytes accessed | tf_op | source)
XLA Modules:
  0.0 141.8 jit_solution(17230677744913810243)
XLA Ops:
  0.6 1.7 %reshape.19.refs_6_ = bf16[48,1152]{1,0:T(8,128)(2,1)} reshape(bf16[48,2,576]{2,1,0:T(2,128)(2,1)} %param.14) | data formatting | bytes 221184 | tf_op jit(solution)/shard_map/reshape | solution.py:1317
  2.3 130.5 %shard_map.161 = (f32[512,768]{1,0:T(8,128)}, f32[512,768]{1,0:T(8,128)}, f32[3,48,384]{2,1,0:T(8,128)}, f32[48,384]{1,0:T(8,128)}, f32[48,576]{1,0:T(8,128)}, /...) custom-call(s32[1,16]{1,0:T(1,128)} %refs_0_.1, f32[512,768]{1,0:T(8,128)} %refs_1_.1, f32[512,768]{1,0:T(8,128)} %refs_2_.1, ...), custom_call_target="tpu_custom_call" | custom-call | flops 12000000000 | bytes 30000000 | tf_op jit(solution)/shard_map/pallas_call | solution.py:1293
  132.9 1.2 slice_bitcast_fusion
  134.1 1.0 pad_maximum_fusion
  135.1 0.8 copy.18
  135.9 0.0 copy-start
  135.9 2.8 %copy.24 = f32[512,768]{1,0:T(8,128)} copy(f32[512,768]{1,0:T(8,128)} %get-tuple-element.42) | data formatting | bytes 3145728
  138.7 0.0 copy-done
  138.7 0.0 copy-start.1
  138.7 0.0 copy-start.3
  138.7 0.0 copy-start.2
  138.7 1.1 copy.25
  139.8 0.0 copy-done.1
  139.8 0.7 copy.26
  140.5 0.0 copy-done.3
  140.5 0.6 copy.27
  141.2 0.0 copy-done.2
  141.2 0.6 copy.28
Async XLA Ops:
  135.9 2.8 %copy-start = (f32[512,768]{1,0:T(8,128)S(1)}, f32[512,768]{1,0:T(8,128)}, u32[]{:S(2)}) copy-start(f32[512,768]{1,0:T(8,128)} %get-tuple-element.43) | copy-start | bytes 4718596
  138.7 1.2 copy-start.1
  138.7 1.8 %copy-start.3 = (f32[48,384]{1,0:T(8,128)S(1)}, f32[48,384]{1,0:T(8,128)}, u32[]{:S(2)}) copy-start(f32[48,384]{1,0:T(8,128)} %get-tuple-element.19) | copy-start | bytes 221188
  138.7 2.5 %copy-start.2 = (f32[48,576]{1,0:T(8,128)S(1)}, f32[48,576]{1,0:T(8,128)}, u32[]{:S(2)}) copy-start(f32[48,576]{1,0:T(8,128)} %get-tuple-element.22) | copy-start | bytes 331780
